TPU v7x, 32 devices: a whole 2x2x4 slice. The times are simulated.
32 devices in a mesh: section: 2 (over core), dp: 16 (over z, y, x).
Axes of the slice: x: 2, y: 2, z: 4, core: 2. Of those that a mesh axis runs over, the one named last changes fastest.
Arguments:
- input_big: bfloat16 [2, 32, 197, 768], P(None, 'dp'), may hold values from -6 to 6
- input_small: bfloat16 [2, 64, 37, 768], P(None, 'dp'), may hold values from -6 to 6
- small_counts: int32 [2, 16], P(None, 'dp'), may hold values from 1 to 4, as said below
- cotangent_big: bfloat16 [2, 32, 197, 768], P(None, 'dp'), may hold values from -6 to 6
- cotangent_small: bfloat16 [2, 64, 37, 768], P(None, 'dp'), may hold values from -6 to 6
- norm1_gain: float32 [2, 768], P('section'), may hold values from 0.5 to 1.5
- norm1_bias: float32 [2, 768], P('section'), may hold values from -1.75 to 1.75
- qkv_weight: bfloat16 [2, 768, 2304], P('section'), may hold values from -0.21875 to 0.21875
- query_bias: float32 [2, 768], P('section'), may hold values from -1.75 to 1.75
- value_bias: float32 [2, 768], P('section'), may hold values from -1.75 to 1.75
- table_big: float32 [2, 732, 12], P('section'), may hold values from -3 to 3
- table_small: float32 [2, 124, 12], P('section'), may hold values from -3 to 3
- proj_weight: bfloat16 [2, 768, 768], P('section'), may hold values from -1.25 to 1.25
- proj_bias: float32 [2, 768], P('section'), may hold values from -1.75 to 1.75
- attn_scale: float32 [2, 768], P('section'), may hold values from 0.5 to 1.5
- norm2_gain: float32 [2, 768], P('section'), may hold values from 0.5 to 1.5
- norm2_bias: float32 [2, 768], P('section'), may hold values from -1.75 to 1.75
- up_weight: bfloat16 [2, 768, 3072], P('section'), may hold values from -0.21875 to 0.21875
- up_bias: float32 [2, 3072], P('section'), may hold values from -1.75 to 1.75
- down_weight: bfloat16 [2, 3072, 768], P('section'), may hold values from -0.109375 to 0.109375
- down_bias: float32 [2, 768], P('section'), may hold values from -1.75 to 1.75
- mlp_scale: float32 [2, 768], P('section'), may hold values from 0.5 to 1.5
Outputs:
- layer_big: bfloat16 [2, 2, 32, 197, 768], P('section', None, 'dp')
- layer_small: bfloat16 [2, 2, 64, 37, 768], P('section', None, 'dp')
- input_grad_big: bfloat16 [2, 2, 32, 197, 768], P('section', None, 'dp')
- input_grad_small: bfloat16 [2, 2, 64, 37, 768], P('section', None, 'dp')
- grad_norm1_gain: float32 [2, 768], P('section', 'dp')
- grad_norm1_bias: float32 [2, 768], P('section', 'dp')
- grad_qkv_weight: float32 [2, 768, 2304], P('section', 'dp')
- grad_query_bias: float32 [2, 768], P('section', 'dp')
- grad_value_bias: float32 [2, 768], P('section', 'dp')
- grad_table_big: float32 [2, 732, 12], P('section')
- grad_table_small: float32 [2, 124, 12], P('section')
- grad_proj_weight: float32 [2, 768, 768], P('section', 'dp')
- grad_proj_bias: float32 [2, 768], P('section', 'dp')
- grad_attn_scale: float32 [2, 768], P('section', 'dp')
- grad_norm2_gain: float32 [2, 768], P('section', 'dp')
- grad_norm2_bias: float32 [2, 768], P('section', 'dp')
- grad_up_weight: float32 [2, 768, 3072], P('section', 'dp')
- grad_up_bias: float32 [2, 3072], P('section', 'dp')
- grad_down_weight: float32 [2, 3072, 768], P('section', 'dp')
- grad_down_bias: float32 [2, 768], P('section', 'dp')
- grad_mlp_scale: float32 [2, 768], P('section', 'dp')
Inputs may be any that keep to these rules, and one draw needn't show every extreme that they name: `small_counts`: each image's number of live small crop slots (the first ones of its 4); some image has 4 and some has 1.
All inputs are finite; a program needn't handle non-finite values.
Results may differ from a plain program's by a relative error of at most 0.018.
Values may be sent and summed in bfloat16 or wider, within the bound.
No kernel may reach another device: no remote copies, remote signals or barrier semaphores. Data moves between devices by JAX's collectives and lax.ppermute only.
A program may use at most 320 MiB of HBM per device.

v0:
```python
import math

import jax
import jax.numpy as jnp
from jax import lax
from jax.sharding import PartitionSpec as P

HEADS = 12


def from_behind(shard, axis, by):
    devices = lax.axis_size(axis)
    pairs = [(i, i + by) for i in range(devices) if 0 <= i + by < devices]
    return lax.ppermute(shard, axis, pairs)


def layer_norm(values, gain, shift):
    centre = values - jnp.mean(values, axis=-1, keepdims=True)
    spread = jnp.mean(centre * centre, axis=-1, keepdims=True)
    return centre * lax.rsqrt(spread + 1e-06) * gain + shift


def exact_gelu(values):
    return jax.nn.gelu(values, approximate=False)


def rel_index(grid):
    count = grid * grid
    side = 2 * grid - 1
    places = jnp.arange(count, dtype=jnp.int32)
    across = places // grid
    along = places % grid
    inner = (across[:, None] - across[None, :] + grid - 1) * side + (
        along[:, None] - along[None, :] + grid - 1
    )
    entries = side * side + 3
    table = jnp.zeros((count + 1, count + 1), jnp.int32)
    table = table.at[1:, 1:].set(inner)
    table = table.at[0, :].set(entries - 3)
    table = table.at[:, 0].set(entries - 2)
    table = table.at[0, 0].set(entries - 1)
    return table


def outer_sum(left, right):
    return lax.dot_general(
        left, right, (((0,), (0,)), ((), ())), preferred_element_type=jnp.float32
    )


def back_mult(upstream, weight):
    return lax.dot_general(
        upstream, weight, (((1,), (1,)), ((), ())), preferred_element_type=jnp.float32
    )


def head_parts(projected):
    crops, length, triple = projected.shape
    head = triple // 3 // HEADS
    parts = projected.reshape(crops, length, 3, HEADS, head)
    return (parts[:, :, 0], parts[:, :, 1], parts[:, :, 2], head)


def score_block(query, keys, table, index, head):
    bias = jnp.transpose(jnp.take(table, index, axis=0), (2, 0, 1))
    scores = jnp.einsum("clhd,cmhd->chlm", query, keys, preferred_element_type=jnp.float32)
    return scores * head ** (-0.5) + bias[None]


def attend_forward(projected, table, index):
    query, keys, values, head = head_parts(projected)
    scores = score_block(query, keys, table, index, head)
    highest = jnp.max(scores, axis=-1, keepdims=True)
    raised = jnp.exp(scores - highest)
    summed = jnp.sum(raised, axis=-1, keepdims=True)
    probs = raised / summed
    result = jnp.einsum(
        "chlm,cmhd->clhd", probs.astype(jnp.bfloat16), values, preferred_element_type=jnp.float32
    )
    return (result.reshape(result.shape[0] * result.shape[1], -1), highest + jnp.log(summed))


def attend_backward(projected, log_total, upstream, table, index):
    query, keys, values, head = head_parts(projected)
    crops, length = (projected.shape[0], projected.shape[1])
    scores = score_block(query, keys, table, index, head)
    probs = jnp.exp(scores - log_total)
    incoming = upstream.reshape(crops, length, HEADS, head)
    grad_probs = jnp.einsum("clhd,cmhd->chlm", incoming, values, preferred_element_type=jnp.float32)
    inner = jnp.sum(probs * grad_probs, axis=-1, keepdims=True)
    grad_scores = (probs * (grad_probs - inner)).astype(jnp.bfloat16)
    grad_query = jnp.einsum(
        "chlm,cmhd->clhd", grad_scores, keys, preferred_element_type=jnp.float32
    ) * head ** (-0.5)
    grad_keys = jnp.einsum(
        "chlm,clhd->cmhd", grad_scores, query, preferred_element_type=jnp.float32
    ) * head ** (-0.5)
    grad_values = jnp.einsum(
        "chlm,clhd->cmhd", probs.astype(jnp.bfloat16), incoming, preferred_element_type=jnp.float32
    )
    grad_projected = jnp.stack([grad_query, grad_keys, grad_values], axis=2).reshape(
        crops * length, -1
    )
    summed = jnp.sum(grad_scores.astype(jnp.float32), axis=0).reshape(HEADS, -1)
    grad_table = jax.ops.segment_sum(summed.T, index.reshape(-1), num_segments=table.shape[0])
    return (grad_projected.astype(jnp.bfloat16), grad_table)


def layer_forward(rows, keep, weights, layout):
    (
        norm1_gain,
        norm1_bias,
        qkv_weight,
        query_bias,
        value_bias,
        table_big,
        table_small,
        proj_weight,
        proj_bias,
        attn_scale,
        norm2_gain,
        norm2_bias,
        up_weight,
        up_bias,
        down_weight,
        down_bias,
        mlp_scale,
    ) = weights
    crops_big, len_big, crops_small, len_small, index_big, index_small = layout
    split = crops_big * len_big
    normed = layer_norm(rows, norm1_gain, norm1_bias).astype(jnp.bfloat16)
    joined_bias = jnp.concatenate([query_bias, jnp.zeros_like(query_bias), value_bias])
    projected = (
        jnp.dot(normed, qkv_weight, preferred_element_type=jnp.float32) + joined_bias
    ).astype(jnp.bfloat16)
    big, log_big = attend_forward(
        projected[:split].reshape(crops_big, len_big, -1), table_big, index_big
    )
    small, log_small = attend_forward(
        projected[split:].reshape(crops_small, len_small, -1), table_small, index_small
    )
    attended = jnp.concatenate([big, small], axis=0).astype(jnp.bfloat16)
    branch = jnp.dot(attended, proj_weight, preferred_element_type=jnp.float32) + proj_bias
    middle = rows + attn_scale * branch
    normed2 = layer_norm(middle, norm2_gain, norm2_bias).astype(jnp.bfloat16)
    pre = jnp.dot(normed2, up_weight, preferred_element_type=jnp.float32) + up_bias
    hidden = exact_gelu(pre).astype(jnp.bfloat16)
    mlp = jnp.dot(hidden, down_weight, preferred_element_type=jnp.float32) + down_bias
    result = (middle + mlp_scale * mlp) * keep[:, None]
    saved = (
        rows,
        normed,
        projected,
        log_big,
        log_small,
        attended,
        branch,
        middle,
        normed2,
        pre,
        hidden,
        mlp,
        keep,
    )
    return (result, saved)


def mlp_backward(upstream, saved, weights):
    norm2_gain, norm2_bias, up_weight, down_weight, mlp_scale = (
        weights[10],
        weights[11],
        weights[12],
        weights[14],
        weights[16],
    )
    (
        rows,
        normed,
        projected,
        log_big,
        log_small,
        attended,
        branch,
        middle,
        normed2,
        pre,
        hidden,
        mlp,
        keep,
    ) = saved
    upstream = upstream * keep[:, None]
    grad_mlp_scale = jnp.sum(upstream * mlp, axis=0)
    grad_mlp = (mlp_scale * upstream).astype(jnp.bfloat16)
    grad_down_bias = jnp.sum(grad_mlp.astype(jnp.float32), axis=0)
    grad_down_weight = outer_sum(hidden, grad_mlp)
    unused, gelu_back = jax.vjp(exact_gelu, pre)
    grad_pre = gelu_back(back_mult(grad_mlp, down_weight))[0].astype(jnp.bfloat16)
    grad_up_bias = jnp.sum(grad_pre.astype(jnp.float32), axis=0)
    grad_up_weight = outer_sum(normed2, grad_pre)
    unused, norm_back = jax.vjp(layer_norm, middle, norm2_gain, norm2_bias)
    grad_middle, grad_norm2_gain, grad_norm2_bias = norm_back(back_mult(grad_pre, up_weight))
    grad_middle = grad_middle + upstream
    return (
        grad_middle,
        (
            grad_norm2_gain,
            grad_norm2_bias,
            grad_up_weight,
            grad_up_bias,
            grad_down_weight,
            grad_down_bias,
            grad_mlp_scale,
        ),
    )


def attention_backward(grad_middle, saved, weights, layout):
    (
        norm1_gain,
        norm1_bias,
        qkv_weight,
        query_bias,
        value_bias,
        table_big,
        table_small,
        proj_weight,
        proj_bias,
        attn_scale,
    ) = weights[:10]
    crops_big, len_big, crops_small, len_small, index_big, index_small = layout
    (
        rows,
        normed,
        projected,
        log_big,
        log_small,
        attended,
        branch,
        middle,
        normed2,
        pre,
        hidden,
        mlp,
        keep,
    ) = saved
    split = crops_big * len_big
    width = rows.shape[1]
    grad_attn_scale = jnp.sum(grad_middle * branch, axis=0)
    grad_branch = (attn_scale * grad_middle).astype(jnp.bfloat16)
    grad_proj_bias = jnp.sum(grad_branch.astype(jnp.float32), axis=0)
    grad_proj_weight = outer_sum(attended, grad_branch)
    grad_attended = back_mult(grad_branch, proj_weight).astype(jnp.bfloat16)
    big_part, grad_table_big = attend_backward(
        projected[:split].reshape(crops_big, len_big, -1),
        log_big,
        grad_attended[:split],
        table_big,
        index_big,
    )
    small_part, grad_table_small = attend_backward(
        projected[split:].reshape(crops_small, len_small, -1),
        log_small,
        grad_attended[split:],
        table_small,
        index_small,
    )
    grad_projected = jnp.concatenate([big_part, small_part], axis=0)
    grad_query_bias = jnp.sum(grad_projected[:, :width].astype(jnp.float32), axis=0)
    grad_value_bias = jnp.sum(grad_projected[:, 2 * width :].astype(jnp.float32), axis=0)
    grad_qkv_weight = outer_sum(normed, grad_projected)
    unused, norm_back = jax.vjp(layer_norm, rows, norm1_gain, norm1_bias)
    grad_rows, grad_norm1_gain, grad_norm1_bias = norm_back(back_mult(grad_projected, qkv_weight))
    grads = (
        grad_norm1_gain,
        grad_norm1_bias,
        grad_qkv_weight,
        grad_query_bias,
        grad_value_bias,
        grad_table_big,
        grad_table_small,
        grad_proj_weight,
        grad_proj_bias,
        grad_attn_scale,
    )
    return (grad_rows + grad_middle, grads)


def layer_backward(upstream, saved, weights, layout):
    grad_middle, mlp_grads = mlp_backward(upstream, saved, weights)
    going_back, attn_grads = attention_backward(grad_middle, saved, weights, layout)
    return (going_back, attn_grads + mlp_grads)


def body(
    input_big,
    input_small,
    small_counts,
    cotangent_big,
    cotangent_small,
    norm1_gain,
    norm1_bias,
    qkv_weight,
    query_bias,
    value_bias,
    table_big,
    table_small,
    proj_weight,
    proj_bias,
    attn_scale,
    norm2_gain,
    norm2_bias,
    up_weight,
    up_bias,
    down_weight,
    down_bias,
    mlp_scale,
):
    weights = tuple(
        (
            item[0]
            for item in (
                norm1_gain,
                norm1_bias,
                qkv_weight,
                query_bias,
                value_bias,
                table_big,
                table_small,
                proj_weight,
                proj_bias,
                attn_scale,
                norm2_gain,
                norm2_bias,
                up_weight,
                up_bias,
                down_weight,
                down_bias,
                mlp_scale,
            )
        )
    )
    micro, crops_big, len_big, width = input_big.shape
    crops_small, len_small = (input_small.shape[1], input_small.shape[2])
    slots = crops_small // small_counts.shape[1]
    split = crops_big * len_big
    layout = (
        crops_big,
        len_big,
        crops_small,
        len_small,
        rel_index(math.isqrt(len_big - 1)),
        rel_index(math.isqrt(len_small - 1)),
    )
    section = lax.axis_index("section")
    first = section == 0
    inputs = jnp.concatenate(
        [
            input_big.reshape(micro, split, width),
            input_small.reshape(micro, crops_small * len_small, width),
        ],
        axis=1,
    )
    cotangent = jnp.concatenate(
        [
            cotangent_big.reshape(micro, split, width),
            cotangent_small.reshape(micro, crops_small * len_small, width),
        ],
        axis=1,
    )

    def rows_keep(batch):
        counts = lax.dynamic_index_in_dim(small_counts, batch, 0, keepdims=False)
        slot_of = jnp.arange(crops_small * len_small, dtype=jnp.int32) // len_small % slots
        small = (slot_of < jnp.repeat(counts, slots * len_small)).astype(jnp.float32)
        return jnp.concatenate([jnp.ones((split,), jnp.float32), small])

    received = jnp.zeros_like(inputs[0])
    kept = [inputs[0]] * micro
    results = [jnp.zeros_like(inputs[0])] * micro
    for step in range(micro + 1):
        batch = step - section
        clipped = jnp.clip(batch, 0, micro - 1)
        entry = jnp.where(first, inputs[min(step, micro - 1)], received)
        outcome, unused = layer_forward(
            entry.astype(jnp.float32), rows_keep(clipped), weights, layout
        )
        sent = outcome.astype(jnp.bfloat16)
        for member in range(micro):
            chosen = batch == member
            results[member] = jnp.where(chosen, sent, results[member])
            kept[member] = jnp.where(chosen, entry, kept[member])
        if step < micro:
            received = from_behind(sent, "section", 1)
    kept_all = jnp.stack(kept)
    arriving = jnp.zeros_like(inputs[0])
    main_index = (0, 1, 2, 3, 4, 7, 8, 9, 10, 11, 12, 13, 14, 15, 16)
    pending = tuple((jnp.zeros(weights[place].shape, jnp.float32) for place in main_index))
    table_totals = (
        jnp.zeros(weights[5].shape, jnp.float32),
        jnp.zeros(weights[6].shape, jnp.float32),
    )
    backward_rows = [jnp.zeros_like(inputs[0])] * micro
    for step in range(micro + 1):
        batch = step - 1 + section
        live = ((batch >= 0) & (batch < micro)).astype(jnp.float32)
        clipped = jnp.clip(batch, 0, micro - 1)
        outer = lax.dynamic_index_in_dim(cotangent, clipped, 0, keepdims=False)
        upstream = jnp.where(first, arriving, outer).astype(jnp.float32) * live
        entry = lax.dynamic_index_in_dim(kept_all, clipped, 0, keepdims=False)
        outcome, saved = layer_forward(
            entry.astype(jnp.float32), rows_keep(clipped), weights, layout
        )
        going_back, grads = layer_backward(upstream, saved, weights, layout)
        pending = tuple((total + grads[place] for total, place in zip(pending, main_index)))
        table_totals = (table_totals[0] + grads[5], table_totals[1] + grads[6])
        sent = going_back.astype(jnp.bfloat16)
        for member in range(micro):
            backward_rows[member] = jnp.where(batch == member, sent, backward_rows[member])
        if step < micro:
            arriving = from_behind(sent, "section", -1)
    shards = (
        lax.psum_scatter(pending[0], "dp", scatter_dimension=0, tiled=True),
        lax.psum_scatter(pending[1], "dp", scatter_dimension=0, tiled=True),
        lax.psum_scatter(pending[2], "dp", scatter_dimension=0, tiled=True),
        lax.psum_scatter(pending[3], "dp", scatter_dimension=0, tiled=True),
        lax.psum_scatter(pending[4], "dp", scatter_dimension=0, tiled=True),
        lax.psum_scatter(pending[5], "dp", scatter_dimension=0, tiled=True),
        lax.psum_scatter(pending[6], "dp", scatter_dimension=0, tiled=True),
        lax.psum_scatter(pending[7], "dp", scatter_dimension=0, tiled=True),
        lax.psum_scatter(pending[8], "dp", scatter_dimension=0, tiled=True),
        lax.psum_scatter(pending[9], "dp", scatter_dimension=0, tiled=True),
        lax.psum_scatter(pending[10], "dp", scatter_dimension=0, tiled=True),
        lax.psum_scatter(pending[11], "dp", scatter_dimension=0, tiled=True),
        lax.psum_scatter(pending[12], "dp", scatter_dimension=0, tiled=True),
        lax.psum_scatter(pending[13], "dp", scatter_dimension=0, tiled=True),
        lax.psum_scatter(pending[14], "dp", scatter_dimension=0, tiled=True),
    )
    tables = lax.psum((table_totals[0], table_totals[1]), "dp")
    stacked = jnp.stack(results)
    stacked_back = jnp.stack(backward_rows)
    layer_big = stacked[:, :split].reshape(micro, crops_big, len_big, width)[None]
    layer_small = stacked[:, split:].reshape(micro, crops_small, len_small, width)[None]
    input_grad_big = stacked_back[:, :split].reshape(micro, crops_big, len_big, width)[None]
    input_grad_small = stacked_back[:, split:].reshape(micro, crops_small, len_small, width)[None]
    return (
        layer_big,
        layer_small,
        input_grad_big,
        input_grad_small,
        shards[0][None],
        shards[1][None],
        shards[2][None],
        shards[3][None],
        shards[4][None],
        tables[0][None],
        tables[1][None],
        shards[5][None],
        shards[6][None],
        shards[7][None],
        shards[8][None],
        shards[9][None],
        shards[10][None],
        shards[11][None],
        shards[12][None],
        shards[13][None],
        shards[14][None],
    )


def solution(mesh):
    in_specs = (
        P(None, "dp", None, None),
        P(None, "dp", None, None),
        P(None, "dp"),
        P(None, "dp", None, None),
        P(None, "dp", None, None),
        P("section", None),
        P("section", None),
        P("section", None, None),
        P("section", None),
        P("section", None),
        P("section", None, None),
        P("section", None, None),
        P("section", None, None),
        P("section", None),
        P("section", None),
        P("section", None),
        P("section", None),
        P("section", None, None),
        P("section", None),
        P("section", None, None),
        P("section", None),
        P("section", None),
    )
    out_specs = (
        P("section", None, "dp", None, None),
        P("section", None, "dp", None, None),
        P("section", None, "dp", None, None),
        P("section", None, "dp", None, None),
        P("section", "dp"),
        P("section", "dp"),
        P("section", "dp", None),
        P("section", "dp"),
        P("section", "dp"),
        P("section", None, None),
        P("section", None, None),
        P("section", "dp", None),
        P("section", "dp"),
        P("section", "dp"),
        P("section", "dp"),
        P("section", "dp"),
        P("section", "dp", None),
        P("section", "dp"),
        P("section", "dp", None),
        P("section", "dp"),
        P("section", "dp"),
    )
    return jax.shard_map(body, mesh=mesh, in_specs=in_specs, out_specs=out_specs, check_vma=False)
```

profile of v0, /device:TPU:0, one launch (start us, length us, event | category | flops | bytes accessed | tf_op | source)
XLA Modules:
  0.0 2412.0 jit_solution(17011535819314850348)
XLA Ops:
  109.0 142.2 %gather_fusion = f32[38809,12]{1,0:T(8,128)} fusion(f32[732,12]{1,0:T(8,128)} %bitcast.703, s32[38912]{0:T(1024)} %pad_clamp_fusion), kind=kCustom, calls=%fused_computation.clone | custom fusion | bytes 3880900 | tf_op jit(solution)/shard_map/jit(_take)/gather | solution.py:65
  251.2 12.1 copy.271
  293.1 17.4 multiply_convert_fusion.15
  376.2 17.8 multiply_convert_fusion.14
  585.9 49.7 %multiply_convert_fusion = (bf16[542,3072]{1,0:T(8,128)(2,1)}, f32[542,3072]{1,0:T(8,128)}, bf16[542,3072]{1,0:T(8,128)(2,1)}, f32[542,3072]{1,0:T(8,128)}, bf16...) fusion(f32[3072]{0:T(1024)S(1)} %bitcast.742, f32[542,3072]{1,0:T(8,128)S(1)} %fusion.78, ...), kind=kOutput, calls=%fused_computation.35 | convolution fusion | flops 2889232896 | bytes 56357104 | tf_op jit(solution)/shard_map/dot_general | solution.py:146
  635.7 10.2 convert_reduce_fusion.2
  736.0 11.0 copy.386
  747.0 9.7 scatter_custom_fusion.3
  756.8 208.3 %scatter_custom_fusion = f32[732,12]{1,0:T(8,128)} fusion(s32[38809]{0:T(1024)} %reshape.971, f32[38809,12]{1,0:T(8,128)} %copy.386, f32[]{:T(128)} %constant.440.clone.1), kind=kCustom, calls=%fused_computation.725 | custom fusion | flops 465708 | bytes 35648 | tf_op jit(solution)/shard_map/scatter-add | solution.py:105
  973.8 10.2 convert_reduce_fusion.1
  1066.1 9.8 scatter_custom_fusion.4
  1082.9 11.0 copy.388
  1093.8 208.5 %scatter_custom_fusion.1 = f32[732,12]{1,0:T(8,128)} fusion(s32[38809]{0:T(1024)} %reshape.971, f32[38809,12]{1,0:T(8,128)} %copy.388, f32[]{:T(128)} %constant.440.clone.1), kind=kCustom, calls=%fused_computation.723 | custom fusion | flops 465708 | bytes 35648 | tf_op jit(solution)/shard_map/scatter-add | solution.py:105
  1314.3 9.9 convert_reduce_fusion
  1418.4 11.0 copy.390
  1429.4 9.8 scatter_fusion.1
  1442.3 189.2 %scatter_fusion = f32[732,12]{1,0:T(8,128)} fusion(f32[732,12]{1,0:T(8,128)} %add.958, s32[38809]{0:T(1024)} %reshape.971, f32[38809,12]{1,0:T(8,128)} %copy.390), kind=kCustom, calls=%fused_computation.4 | custom fusion | flops 465708 | bytes 5743732 | tf_op jit(solution)/shard_map/scatter-add | solution.py:105
  1687.4 9.7 add_add_fusion.1
  1708.4 10.4 add_add_fusion
  1787.2 18.1 select_bitcast_fusion.3
  1844.0 52.0 %reduce-scatter.7.cloned.1.call-done = f32[48,768]{1,0:T(8,128)} async-done(((f32[768,768]{1,0:T(8,128)}), f32[48,768]{1,0:T(8,128)}) %reduce-scatter.7.cloned.1.call-update) | async-done | bytes 147472 | tf_op jit(solution)/shard_map/reduce_scatter | solution.py:427
  1896.0 156.3 %reduce-scatter.5.cloned.1.call-done = f32[48,2304]{1,0:T(8,128)} async-done(((f32[768,2304]{1,0:T(8,128)}), f32[48,2304]{1,0:T(8,128)}) %reduce-scatter.5.cloned.1.call-update) | async-done | bytes 442384 | tf_op jit(solution)/shard_map/reduce_scatter | solution.py:424
  2052.3 177.0 %reduce-scatter.9.cloned.1.call-done = f32[48,3072]{1,0:T(8,128)} async-done(((f32[768,3072]{1,0:T(8,128)}), f32[48,3072]{1,0:T(8,128)}) %reduce-scatter.9.cloned.1.call-update) | async-done | bytes 589840 | tf_op jit(solution)/shard_map/reduce_scatter | solution.py:432
  2229.3 175.9 %reduce-scatter.11.cloned.1.call-done = f32[192,768]{1,0:T(8,128)} async-done(((f32[3072,768]{1,0:T(8,128)}), f32[192,768]{1,0:T(8,128)}) %reduce-scatter.11.cloned.1.call-update) | async-done | bytes 589840 | tf_op jit(solution)/shard_map/reduce_scatter | solution.py:434
  (1019 shorter events, 855.8 us)
Async XLA Ops:
  7.2 31.2 %copy-start = (bf16[1,768,2304]{2,1,0:T(8,128)(2,1)S(1)}, bf16[1,768,2304]{2,1,0:T(8,128)(2,1)}, u32[]{:S(2)}) copy-start(bf16[1,768,2304]{2,1,0:T(8,128)(2,1)} %param.49) | copy-start | bytes 10616836
  7.2 1819.6 %all-reduce.22.cloned.1.call-start = ((), (), s32[]{:S(2)}) async-start(), calls=%async_computation.8 | async-start | bytes 991232
  43.2 327.8 %copy-start.132 = (f32[768]{0:T(1024)}, f32[768]{0:T(1024)S(1)}, u32[]{:S(2)}) copy-start(f32[768]{0:T(1024)S(1)} %reduce.36) | copy-start | bytes 9220
  43.2 249.8 %copy-start.194 = (f32[768]{0:T(1024)}, f32[768]{0:T(1024)S(1)}, u32[]{:S(2)}) copy-start(f32[768]{0:T(1024)S(1)} %reduce.35) | copy-start | bytes 9220
  43.9 327.1 %copy-start.136 = (f32[768]{0:T(1024)}, f32[768]{0:T(1024)S(1)}, u32[]{:S(2)}) copy-start(f32[768]{0:T(1024)S(1)} %reduce.37) | copy-start | bytes 9220
  44.6 322.9 %copy-start.182 = (f32[768]{0:T(1024)}, f32[768]{0:T(1024)S(1)}, u32[]{:S(2)}) copy-start(f32[768]{0:T(1024)S(1)} %reduce.29) | copy-start | bytes 9220
  293.1 20.0 copy-start.257
  293.1 21.9 copy-start.40
  293.1 21.9 copy-start.72
  310.5 4.5 collective-permute-start
  394.0 20.1 collective-permute-start.1
  585.9 49.8 %copy-start.267 = (f32[542,3072]{1,0:T(8,128)}, f32[542,3072]{1,0:T(8,128)S(1)}, u32[]{:S(2)}) copy-start(f32[542,3072]{1,0:T(8,128)S(1)} %fusion.78) | copy-start | bytes 19980292
  585.9 49.8 %copy-start.68 = (bf16[1,542,768]{2,1,0:T(8,128)(2,1)S(1)}, bf16[1,542,768]{2,1,0:T(8,128)(2,1)}, u32[]{:S(2)}) copy-start(bf16[1,542,768]{2,1,0:T(8,128)(2,1)} %fusion.348) | copy-start | bytes 2497540
  585.9 49.8 %copy-start.196 = (f32[768]{0:T(1024)S(1)}, f32[768]{0:T(1024)}, u32[]{:S(2)}) copy-start(f32[768]{0:T(1024)} %copy-done.194) | copy-start | bytes 9220
  585.9 49.8 %copy-start.218 = (f32[542]{0:T(1024)S(1)}, f32[542]{0:T(1024)}, u32[]{:S(2)}) copy-start(f32[542]{0:T(1024)} %pad_convert_fusion.2) | copy-start | bytes 6508
  720.8 251.3 %collective-permute-start.2 = (bf16[542,768]{1,0:T(8,128)(2,1)}, bf16[542,768]{1,0:T(8,128)(2,1)}, u32[]{:S(2)}, u32[]{:S(2)}) collective-permute-start(bf16[542,768]{1,0:T(8,128)(2,1)} %get-tuple-element.298), channel_id=1, source_target_pairs={{16,0},{17,1},{18,2},{19,3},{20,4},{21,5},{22,6},{23,7},{24,8},{25... | collective-permute-start | bytes 2497544 | tf_op jit(solution)/shard_map/ppermute | solution.py:14
  736.0 229.0 %copy-start.220 = (f32[542]{0:T(1024)S(1)}, f32[542]{0:T(1024)}, u32[]{:S(2)}) copy-start(f32[542]{0:T(1024)} %pad_convert_fusion.2) | copy-start | bytes 6508
  1057.9 254.9 %collective-permute-start.3 = (bf16[542,768]{1,0:T(8,128)(2,1)}, bf16[542,768]{1,0:T(8,128)(2,1)}, u32[]{:S(2)}, u32[]{:S(2)}) collective-permute-start(bf16[542,768]{1,0:T(8,128)(2,1)} %add_convert_fusion.10), channel_id=1, source_target_pairs={{16,0},{17,1},{18,2},{19,3},{20,4},{21,5},{22,6},{23,7},{24,8},{25... | collective-permute-start | bytes 2497544 | tf_op jit(solution)/shard_map/ppermute | solution.py:14
  1305.7 18.5 slice-start.10
  1418.4 20.8 copy-start.190
  1645.7 250.3 %reduce-scatter.7.cloned.1.call-start = ((), (), s32[]{:S(2)}) async-start(), calls=%async_computation.5 | async-start | bytes 2506752 | tf_op jit(solution)/shard_map/reduce_scatter | solution.py:427
  1651.4 400.9 %reduce-scatter.5.cloned.1.call-start = ((), (), s32[]{:S(2)}) async-start(), calls=%async_computation.4 | async-start | bytes 7520256 | tf_op jit(solution)/shard_map/reduce_scatter | solution.py:424
  1673.0 556.2 %reduce-scatter.9.cloned.1.call-start = ((), (), s32[]{:S(2)}) async-start(), calls=%async_computation.6 | async-start | bytes 10027008 | tf_op jit(solution)/shard_map/reduce_scatter | solution.py:432
  1697.1 708.1 %reduce-scatter.11.cloned.1.call-start = ((), (), s32[]{:S(2)}) async-start(), calls=%async_computation.7 | async-start | bytes 10027008 | tf_op jit(solution)/shard_map/reduce_scatter | solution.py:434
  (272 other events, 1108.7 us)
Sparse Core Ops, SparseCore 0:
  1645.9 117.6 all-reduce.21
  1769.1 126.8 reduce-scatter.6
  1902.8 149.4 reduce-scatter.4
  2059.4 169.8 reduce-scatter.8
  2235.4 169.7 reduce-scatter.10
where the time goes:
time: 2430 us; the launch traced here: 2410 us
  other arithmetic  779 us (32%)
  local copies, waits for them, and re-layouts  640 us (26%)
  waiting for transfers between devices  562 us (23%)
  matrix products  403 us (17%)
    scatter-add x6, other arithmetic, attend_backward(): jax.ops.segment_sum(summed.T, index.reshape(-1), num_segments=table.shape...  635 us
    reduce_scatter x1, waiting for transfers between devices, body(): lax.psum_scatter(pending[10], 'dp', scatter_dimension=0, tiled=True)  177 us
    reduce_scatter x1, waiting for transfers between devices, body(): lax.psum_scatter(pending[12], 'dp', scatter_dimension=0, tiled=True)  176 us
    gather x6, local copies, waits for them, and re-layouts, score_block(): bias = jnp.transpose(jnp.take(table, index, axis=0), (2, 0, 1))  167 us
    reduce_scatter x1, waiting for transfers between devices, body(): lax.psum_scatter(pending[2], 'dp', scatter_dimension=0, tiled=True)  156 us
    unnamed x606, local copies, waits for them, and re-layouts  90.8 us
    dot_general x12, matrix products, outer_sum(): lax.dot_general(left, right, (((0,), (0,)), ((), ())), preferred_element_...  76.2 us
    dot_general x6, matrix products, layer_forward(): jnp.dot(hidden, down_weight, preferred_element_type=jnp.float32) + down_bias  73.1 us
  transfers between devices with their start and end apart: 9, of which 5 were waited for; matrix products, arithmetic and copies ran while one was open for 30% of the time, Pallas kernels for 0%

commit v1 on v0

v1 whole, which is shorter than its diff:
```python
import math

import jax
import jax.numpy as jnp
from jax import lax
from jax.experimental import pallas as pl
from jax.experimental.pallas import tpu as pltpu
from jax.sharding import PartitionSpec as P

HEADS = 12
EPS = 1e-06
LOW = -1e30
VMEM_BYTES = 56 * 1024 * 1024
F32 = jnp.float32
BF16 = jnp.bfloat16
V = pl.BlockSpec(memory_space=pltpu.VMEM)
S = pl.BlockSpec(memory_space=pltpu.SMEM)
H = pl.BlockSpec(memory_space=pl.ANY)


def up_to(value, multiple):
    return -(-value // multiple) * multiple


def mm(left, right):
    return jnp.dot(left, right, preferred_element_type=F32)


def mm_back(left, right):
    return lax.dot_general(left, right, (((1,), (1,)), ((), ())), preferred_element_type=F32)


def mm_outer(left, right):
    return lax.dot_general(left, right, (((0,), (0,)), ((), ())), preferred_element_type=F32)


def norm_parts(values):
    centre = values - jnp.mean(values, axis=-1, keepdims=True)
    spread = jnp.mean(centre * centre, axis=-1, keepdims=True)
    scale = lax.rsqrt(spread + EPS)
    return centre * scale, scale


def norm_back(upstream, values, gain):
    unit, scale = norm_parts(values)
    scaled = upstream * gain
    first = jnp.mean(scaled, axis=-1, keepdims=True)
    second = jnp.mean(scaled * unit, axis=-1, keepdims=True)
    going = scale * (scaled - first - unit * second)
    return (
        going,
        jnp.sum(upstream * unit, axis=0, keepdims=True),
        jnp.sum(upstream, axis=0, keepdims=True),
    )


def gelu_parts(x):
    raised = jnp.exp(-0.5 * x * x)
    t = 1.0 / (1.0 + (0.3275911 * math.sqrt(0.5)) * jnp.abs(x))
    poly = t * (
        0.127414796
        + t * (-0.142248368 + t * (0.7107068705 + t * (-0.7265760135 + t * 0.5307027145)))
    )
    half = poly * raised
    phi = jnp.where(x >= 0, 1.0 - half, half)
    return x * phi, phi + x * (raised * (1.0 / math.sqrt(2.0 * math.pi)))


def column_cuts(width, parts):
    step = width // parts
    return [(slice(None), pl.ds(i * step, step)) for i in range(parts)]


def row_cuts(height, parts):
    step = height // parts
    return [(pl.ds(i * step, step), slice(None)) for i in range(parts)]


def fetch_start(mine, own, other, buffer, sems, cuts):
    for i, cut in enumerate(cuts):

        @pl.when(mine)
        def _():
            pltpu.make_async_copy(own.at[cut], buffer.at[cut], sems.at[i]).start()

        @pl.when(jnp.logical_not(mine))
        def _():
            pltpu.make_async_copy(other.at[cut], buffer.at[cut], sems.at[i]).start()


def fetch_wait(own, buffer, sems, cuts, i):
    pltpu.make_async_copy(own.at[cuts[i]], buffer.at[cuts[i]], sems.at[i]).wait()


def kernel_call(body, ins, outs, scratch, args, flops, **more):
    moved = sum(math.prod(a.shape) * a.dtype.itemsize for a in args) + sum(
        math.prod(o.shape) * o.dtype.itemsize for o in outs
    )
    return pl.pallas_call(
        body,
        in_specs=ins,
        out_specs=[V] * len(outs),
        out_shape=outs,
        scratch_shapes=scratch,
        compiler_params=pltpu.CompilerParams(vmem_limit_bytes=VMEM_BYTES, **more),
        cost_estimate=pl.CostEstimate(flops=flops, bytes_accessed=moved, transcendentals=0),
    )(*args)


def shape(dims, kind):
    return jax.ShapeDtypeStruct(dims, kind)


def qkv_forward(layer, core, x, gain, shift, joined, own, other):
    rows, width = x.shape
    triple = own.shape[1]
    cuts = column_cuts(triple, 3)

    def body(core_ref, x_ref, gain_ref, shift_ref, joined_ref, own_ref, other_ref, normed_ref, proj_ref, buf, sems):
        mine = core_ref[0] == layer
        fetch_start(mine, own_ref, other_ref, buf, sems, cuts)
        unit, _ = norm_parts(x_ref[...].astype(F32))
        normed_ref[...] = (unit * gain_ref[...] + shift_ref[...]).astype(BF16)
        for i in range(3):
            fetch_wait(own_ref, buf, sems, cuts, i)
            cols = pl.ds(i * width, width)
            proj_ref[:, cols] = (mm(normed_ref[...], buf[:, cols]) + joined_ref[:, cols]).astype(BF16)

    return kernel_call(
        body,
        [S, V, V, V, V, H, H],
        [shape((rows, width), BF16), shape((rows, triple), BF16)],
        [pltpu.VMEM((width, triple), BF16), pltpu.SemaphoreType.DMA((3,))],
        (core, x, gain, shift, joined, own, other),
        2 * rows * width * triple,
    )


def build_bias(base, out_ref, block_ref, grid, corner, crops, length, block_rows):
    lanes = base.shape[1]
    head_patch, patch_head, head_head = corner
    lane = lax.broadcasted_iota(jnp.int32, (block_rows, 256), 1)
    line = lax.broadcasted_iota(jnp.int32, (block_rows, 256), 0)
    first = jnp.where(lane == 0, head_head, head_patch)
    block_ref[...] = jnp.where(lane >= length, LOW, first)
    small = lane[:grid]
    for r in range(grid):
        off = (grid - 1 - r) * grid
        moved = base if off == 0 else pltpu.roll(base, lanes - off, 1)
        moved = moved[:grid, :256]
        value = jnp.where(small == 0, patch_head, jnp.where(small >= length, LOW, moved))
        block_ref[pl.ds(1 + grid * r, grid), :] = value
    if crops == 1:
        return
    out_ref[...] = jnp.full(out_ref.shape, LOW, F32)
    for s in range(crops):
        value = block_ref[pl.ds(0, length), :]
        if s:
            value = pltpu.roll(value, s * length, 1)
        out_ref[pl.ds(s * length, length), :] = value


def attention_forward(projected, base_big, base_small, corners, sizes):
    rows, triple = projected.shape
    width = triple // 3
    pairs = HEADS // 2
    crops, len_big, pad_big, slots, len_small, pad_small = sizes
    grid_big, grid_small = math.isqrt(len_big - 1), math.isqrt(len_small - 1)

    def body(corner_ref, q_ref, k_ref, v_ref, bb_ref, bs_ref, out_ref, big, block, small):
        pair = pl.program_id(0)
        lane = lax.broadcasted_iota(jnp.int32, (1, 128), 1)
        for h in range(2):
            head = pair * 2 + h
            take = (lane // 64) == h
            build_bias(bb_ref[h], big, big, grid_big, [corner_ref[0, i, head] for i in range(3)], 1, len_big, pad_big)
            build_bias(bs_ref[h], small, block, grid_small, [corner_ref[1, i, head] for i in range(3)], slots, len_small, block.shape[0])

            def one(start, count, bias):
                part = pl.ds(start, count)
                q = jnp.where(take, q_ref[part, :], 0)
                scores = mm_back(q, k_ref[part, :]) * 0.125 + bias[:, :count]
                raised = jnp.exp(scores - jnp.max(scores, axis=-1, keepdims=True))
                probs = raised / jnp.sum(raised, axis=-1, keepdims=True)
                result = mm(probs.astype(BF16), v_ref[part, :]).astype(BF16)
                if h == 0:
                    out_ref[part, :] = result
                else:
                    out_ref[part, :] = jnp.where(take, result, out_ref[part, :])

            for crop in range(crops):
                one(crop * pad_big, pad_big, big)
            one(crops * pad_big, pad_small, small)

    return pl.pallas_call(
        body,
        grid=(pairs,),
        in_specs=[
            S,
            pl.BlockSpec((rows, 128), lambda p: (0, p)),
            pl.BlockSpec((rows, 128), lambda p: (0, pairs + p)),
            pl.BlockSpec((rows, 128), lambda p: (0, 2 * pairs + p)),
            pl.BlockSpec((2,) + base_big.shape[1:], lambda p: (p, 0, 0)),
            pl.BlockSpec((2,) + base_small.shape[1:], lambda p: (p, 0, 0)),
        ],
        out_specs=pl.BlockSpec((rows, 128), lambda p: (0, p)),
        out_shape=shape((rows, width), BF16),
        scratch_shapes=[
            pltpu.VMEM((pad_big, 256), F32),
            pltpu.VMEM((up_to(len_small, 8), 256), F32),
            pltpu.VMEM((pad_small, 256), F32),
        ],
        compiler_params=pltpu.CompilerParams(vmem_limit_bytes=VMEM_BYTES),
        cost_estimate=pl.CostEstimate(flops=8 * 10**9, bytes_accessed=4 * rows * width * 2, transcendentals=0),
    )(corners, projected, projected, projected, base_big, base_small)


FF_STEP = 512


def up_forward(layer, core, attended, x, vec, up_bias, own, other, own_up, other_up):
    rows, width = x.shape
    hidden = own_up.shape[1]
    count = hidden // FF_STEP
    cuts = [(slice(None), slice(None))]
    up_cuts = column_cuts(hidden, count)

    def body(core_ref, att_ref, x_ref, vec_ref, bias_ref, own_ref, other_ref, own_up_ref, other_up_ref, branch_ref, middle_ref, normed_ref, hidden_ref, slope_ref, buf, buf_up, sems, sems_up):
        mine = core_ref[0] == layer
        fetch_start(mine, own_ref, other_ref, buf, sems, cuts)
        fetch_start(mine, own_up_ref, other_up_ref, buf_up, sems_up, up_cuts)
        fetch_wait(own_ref, buf, sems, cuts, 0)
        branch = mm(att_ref[...], buf[...]) + vec_ref[4:5, :]
        branch_ref[...] = branch
        middle = x_ref[...].astype(F32) + vec_ref[5:6, :] * branch
        middle_ref[...] = middle
        unit, _ = norm_parts(middle)
        normed_ref[...] = (unit * vec_ref[6:7, :] + vec_ref[7:8, :]).astype(BF16)
        for i in range(count):
            fetch_wait(own_up_ref, buf_up, sems_up, up_cuts, i)
            cols = pl.ds(i * FF_STEP, FF_STEP)
            pre = mm(normed_ref[...], buf_up[:, cols]) + bias_ref[:, cols]
            value, slope = gelu_parts(pre)
            hidden_ref[:, cols] = value.astype(BF16)
            slope_ref[:, cols] = slope.astype(BF16)

    return kernel_call(
        body,
        [S, V, V, V, V, H, H, H, H],
        [
            shape((rows, width), F32),
            shape((rows, width), F32),
            shape((rows, width), BF16),
            shape((rows, hidden), BF16),
            shape((rows, hidden), BF16),
        ],
        [
            pltpu.VMEM((width, width), BF16),
            pltpu.VMEM((width, hidden), BF16),
            pltpu.SemaphoreType.DMA((1,)),
            pltpu.SemaphoreType.DMA((count,)),
        ],
        (core, attended, x, vec, up_bias, own, other, own_up, other_up),
        2 * rows * width * (width + hidden),
    )


def down_forward(layer, core, hidden, middle, keep, vec, own, other):
    rows, width = middle.shape
    depth = hidden.shape[1]
    cuts = row_cuts(depth, 2)
    half = depth // 2

    def body(core_ref, hidden_ref, middle_ref, keep_ref, vec_ref, own_ref, other_ref, y_ref, mlp_ref, buf, sems):
        fetch_start(core_ref[0] == layer, own_ref, other_ref, buf, sems, cuts)
        total = vec_ref[8:9, :]
        for i in range(2):
            fetch_wait(own_ref, buf, sems, cuts, i)
            part = pl.ds(i * half, half)
            total = total + mm(hidden_ref[:, part], buf[part, :])
        mlp_ref[...] = total
        y_ref[...] = ((middle_ref[...] + vec_ref[9:10, :] * total) * keep_ref[...]).astype(BF16)

    return kernel_call(
        body,
        [S, V, V, V, V, H, H],
        [shape((rows, width), BF16), shape((rows, width), F32)],
        [pltpu.VMEM((depth, width), BF16), pltpu.SemaphoreType.DMA((2,))],
        (core, hidden, middle, keep, vec, own, other),
        2 * rows * width * depth,
    )


def mlp_backward(layer, core, upstream, keep, vec, slope, middle, branch, down, up, proj):
    rows, width = middle.shape
    depth = slope.shape[1]
    count = depth // FF_STEP
    half_cols, half_width = depth // 2, width // 2
    down_cuts, up_cuts = row_cuts(depth, count), column_cuts(depth, count)
    cuts = [(slice(None), slice(None))]

    def body(core_ref, g_ref, keep_ref, vec_ref, slope_ref, middle_ref, branch_ref, od, td, ou, tu, op, tp, gm_ref, gp_ref, gb_ref, ga_ref, gmid_ref, vecs_ref, ups_ref, acc, low, bd, bu, bp, sd, su, sp):
        me = core_ref[0]
        mine = me == layer
        fetch_start(mine, od, td, bd, sd, down_cuts)
        fetch_start(mine, ou, tu, bu, su, up_cuts)
        fetch_start(mine, op, tp, bp, sp, cuts)
        gm = (vec_ref[9:10, :] * (g_ref[...].astype(F32) * keep_ref[...])).astype(BF16)
        low[...] = gm
        gm_ref[me] = gm[:, :half_width]
        gm_ref[1 - me] = gm[:, half_width:]
        vecs_ref[...] = jnp.zeros_like(vecs_ref)
        vecs_ref[4:5, :] = jnp.sum(gm.astype(F32), axis=0, keepdims=True)
        for i in range(count):
            cols = pl.ds(i * FF_STEP, FF_STEP)
            fetch_wait(od, bd, sd, down_cuts, i)
            gp = (mm_back(low[...], bd[cols, :]) * slope_ref[:, cols].astype(F32)).astype(BF16)
            slot = me if 2 * i < count else 1 - me
            gp_ref[slot, :, pl.ds((i * FF_STEP) % half_cols, FF_STEP)] = gp
            ups_ref[:, cols] = jnp.sum(gp.astype(F32), axis=0, keepdims=True)
            fetch_wait(ou, bu, su, up_cuts, i)
            more = mm_back(gp, bu[:, cols])
            if i == 0:
                acc[...] = more
            else:
                acc[...] += more
        going, gain, shift = norm_back(acc[...], middle_ref[...], vec_ref[6:7, :])
        gmid = g_ref[...].astype(F32) * keep_ref[...] + going
        gmid_ref[...] = gmid
        gb = (vec_ref[5:6, :] * gmid).astype(BF16)
        low[...] = gb
        gb_ref[me] = gb[:, :half_width]
        gb_ref[1 - me] = gb[:, half_width:]
        vecs_ref[0:1, :] = gain
        vecs_ref[1:2, :] = shift
        vecs_ref[2:3, :] = jnp.sum(gmid * branch_ref[...], axis=0, keepdims=True)
        vecs_ref[3:4, :] = jnp.sum(gb.astype(F32), axis=0, keepdims=True)
        fetch_wait(op, bp, sp, cuts, 0)
        ga_ref[...] = mm_back(low[...], bp[...]).astype(BF16)

    return kernel_call(
        body,
        [S, V, V, V, V, V, V] + [H] * 6,
        [
            shape((2, rows, half_width), BF16),
            shape((2, rows, half_cols), BF16),
            shape((2, rows, half_width), BF16),
            shape((rows, width), BF16),
            shape((rows, width), F32),
            shape((8, width), F32),
            shape((1, depth), F32),
        ],
        [
            pltpu.VMEM((rows, width), F32),
            pltpu.VMEM((rows, width), BF16),
            pltpu.VMEM((depth, width), BF16),
            pltpu.VMEM((width, depth), BF16),
            pltpu.VMEM((width, width), BF16),
            pltpu.SemaphoreType.DMA((count,)),
            pltpu.SemaphoreType.DMA((count,)),
            pltpu.SemaphoreType.DMA((1,)),
        ],
        (core, upstream, keep, vec, slope, middle, branch) + down + up + proj,
        2 * rows * width * (2 * depth + width),
    )


def attention_backward(core, projected, upstream, base_big, base_small, corners, sizes):
    rows, triple = projected.shape
    width = triple // 3
    pairs = HEADS // 2
    crops, len_big, pad_big, slots, len_small, pad_small = sizes
    grid_big, grid_small = math.isqrt(len_big - 1), math.isqrt(len_small - 1)
    half = 3 * pairs // 2

    def body(core_ref, corner_ref, q_ref, k_ref, v_ref, g_ref, bb_ref, bs_ref, gproj_ref, tb_ref, ts_ref, sums_ref, big, block, small, dbig, dsmall, dblock):
        pair = pl.program_id(0)
        me = core_ref[0]
        lane = lax.broadcasted_iota(jnp.int32, (1, 128), 1)

        def put(which, part, value, h):
            place = which * pairs + pair + half * me
            place = jnp.where(place >= 2 * half, place - 2 * half, place)
            value = value.astype(BF16)
            if h == 0:
                gproj_ref[place, part, :] = value
            else:
                gproj_ref[place, part, :] = jnp.where((lane // 64) == h, value, gproj_ref[place, part, :])

        for h in range(2):
            head = pair * 2 + h
            take = (lane // 64) == h
            build_bias(bb_ref[h], big, big, grid_big, [corner_ref[0, i, head] for i in range(3)], 1, len_big, pad_big)
            build_bias(bs_ref[h], small, block, grid_small, [corner_ref[1, i, head] for i in range(3)], slots, len_small, block.shape[0])

            def one(start, count, bias, dref, first):
                part = pl.ds(start, count)
                q, k, v, g = q_ref[part, :], k_ref[part, :], v_ref[part, :], g_ref[part, :]
                scores = mm_back(jnp.where(take, q, 0), k) * 0.125 + bias[:, :count]
                raised = jnp.exp(scores - jnp.max(scores, axis=-1, keepdims=True))
                probs = raised / jnp.sum(raised, axis=-1, keepdims=True)
                gpr = mm_back(jnp.where(take, g, 0), v)
                inner = jnp.sum(probs * gpr, axis=-1, keepdims=True)
                gs = (probs * (gpr - inner)).astype(BF16)
                if first:
                    dref[:, :count] = gs.astype(F32)
                else:
                    dref[:, :count] += gs.astype(F32)
                put(0, part, mm(gs, k) * 0.125, h)
                put(1, part, mm_outer(gs, q) * 0.125, h)
                put(2, part, mm_outer(probs.astype(BF16), g), h)

            for crop in range(crops):
                one(crop * pad_big, pad_big, big, dbig, crop == 0)
            one(crops * pad_big, pad_small, small, dsmall, True)

            def fold(dref, grid, length, out_ref):
                lanes = out_ref.shape[2]
                wide = lax.broadcasted_iota(jnp.int32, (grid, 256), 1)
                inside = (wide > 0) & (wide < length)
                total = jnp.zeros((grid, lanes), F32)
                for r in range(grid):
                    value = jnp.where(inside, dref[pl.ds(1 + grid * r, grid), :], 0)
                    if lanes > 256:
                        value = jnp.concatenate([value, jnp.zeros((grid, lanes - 256), F32)], axis=1)
                    off = (grid - 1 - r) * grid
                    total = total + (value if off == 0 else pltpu.roll(value, off, 1))
                out_ref[h, :grid, :] = total
                line = lax.broadcasted_iota(jnp.int32, (length, 256), 0)
                spot = lax.broadcasted_iota(jnp.int32, (length, 256), 1)
                value = jnp.where(spot < length, dref[pl.ds(0, length), :], 0)
                out_ref[h, grid : grid + 1, :256] = value[0:1, :]
                out_ref[h, grid + 1 : grid + 2, :256] = jnp.sum(jnp.where(line > 0, value, 0), axis=0, keepdims=True)

            if h == 0:
                tb_ref[...] = jnp.zeros_like(tb_ref)
                ts_ref[...] = jnp.zeros_like(ts_ref)
            fold(dbig, grid_big, len_big, tb_ref)
            total = dsmall[pl.ds(0, len_small), :]
            for s in range(1, slots):
                total = total + pltpu.roll(dsmall[pl.ds(s * len_small, len_small), :], 256 - s * len_small, 1)
            dblock[pl.ds(0, len_small), :] = total
            fold(dblock, grid_small, len_small, ts_ref)
        for n, which in ((0, 0), (1, 2)):
            place = which * pairs + pair + half * me
            place = jnp.where(place >= 2 * half, place - 2 * half, place)
            sums_ref[n : n + 1, :] = jnp.sum(gproj_ref[place].astype(F32), axis=0, keepdims=True)

    tb_shape, ts_shape = (16, 512), (8, 256)

    def clear(*refs):
        @pl.when(pl.program_id(0) == 0)
        def _():
            refs[-3][...] = jnp.zeros_like(refs[-3])
            refs[-2][...] = jnp.zeros_like(refs[-2])
            refs[-1][...] = jnp.zeros_like(refs[-1])

        body(*refs)

    return pl.pallas_call(
        clear,
        grid=(pairs,),
        in_specs=[
            S,
            S,
            pl.BlockSpec((rows, 128), lambda p: (0, p)),
            pl.BlockSpec((rows, 128), lambda p: (0, pairs + p)),
            pl.BlockSpec((rows, 128), lambda p: (0, 2 * pairs + p)),
            pl.BlockSpec((rows, 128), lambda p: (0, p)),
            pl.BlockSpec((2,) + base_big.shape[1:], lambda p: (p, 0, 0)),
            pl.BlockSpec((2,) + base_small.shape[1:], lambda p: (p, 0, 0)),
        ],
        out_specs=[
            pl.BlockSpec((2 * half, rows, 128), lambda p: (0, 0, 0)),
            pl.BlockSpec((2,) + tb_shape, lambda p: (p, 0, 0)),
            pl.BlockSpec((2,) + ts_shape, lambda p: (p, 0, 0)),
            pl.BlockSpec((2, 128), lambda p: (0, p)),
        ],
        out_shape=[
            shape((2 * half, rows, 128), BF16),
            shape((HEADS,) + tb_shape, F32),
            shape((HEADS,) + ts_shape, F32),
            shape((2, width), F32),
        ],
        scratch_shapes=[
            pltpu.VMEM((pad_big, 256), F32),
            pltpu.VMEM((up_to(len_small, 8), 256), F32),
            pltpu.VMEM((pad_small, 256), F32),
            pltpu.VMEM((pad_big, 256), F32),
            pltpu.VMEM((pad_small, 256), F32),
            pltpu.VMEM((up_to(len_small, 8), 256), F32),
        ],
        compiler_params=pltpu.CompilerParams(vmem_limit_bytes=VMEM_BYTES),
        cost_estimate=pl.CostEstimate(flops=20 * 10**9, bytes_accessed=8 * rows * width * 2, transcendentals=0),
    )(core, corners, projected, projected, projected, upstream, base_big, base_small)


def qkv_backward(layer, core, gproj, x, gmid, gain, own, other):
    rows, width = x.shape
    blocks = gproj.shape[0]
    triple = blocks * 128
    cuts = column_cuts(triple, 3)
    group = blocks // 3

    def body(core_ref, gproj_ref, x_ref, gmid_ref, gain_ref, own_ref, other_ref, gx_ref, vecs_ref, buf, acc, sems):
        me = core_ref[0]
        fetch_start(me == layer, own_ref, other_ref, buf, sems, cuts)
        for i in range(3):
            fetch_wait(own_ref, buf, sems, cuts, i)
            places = [n + (blocks // 2) * me for n in range(i * group, (i + 1) * group)]
            places = [jnp.where(place >= blocks, place - blocks, place) for place in places]
            joined = jnp.concatenate([gproj_ref[place] for place in places], axis=1)
            more = mm_back(joined, buf[:, pl.ds(i * width, width)])
            if i == 0:
                acc[...] = more
            else:
                acc[...] += more
        going, gain_sum, shift_sum = norm_back(acc[...], x_ref[...].astype(F32), gain_ref[...])
        gx_ref[...] = (gmid_ref[...] + going).astype(BF16)
        vecs_ref[0:1, :] = gain_sum
        vecs_ref[1:2, :] = shift_sum

    return kernel_call(
        body,
        [S, V, V, V, V, H, H],
        [shape((rows, width), BF16), shape((2, width), F32)],
        [
            pltpu.VMEM((width, triple), BF16),
            pltpu.VMEM((rows, width), F32),
            pltpu.SemaphoreType.DMA((3,)),
        ],
        (core, gproj, x, gmid, gain, own, other),
        2 * rows * width * triple,
    )


def place_of(relative, order):
    place = 0
    for bit in order:
        place = place * 2 + ((relative >> bit) & 1)
    return place


def store_block(keep, send, place, sub, value):
    low = keep.shape[0]

    @pl.when(place < low)
    def _():
        keep[place, sub] = value

    @pl.when(place >= low)
    def _():
        send[place - low, sub] = value


def weight_grad_tall(where, orders, x_own, x_other, g_own, g_other):
    devices = 1 << len(orders[0])
    rows, tall = x_own.shape
    cols = g_own.shape[1]
    step = 384
    block = tall // devices
    pieces = cols // 128

    def body(where_ref, xo, xt, go, gt, *outs):
        at = pl.program_id(0)
        left = jnp.concatenate([xo[...], xt[...]], axis=0)
        right = jnp.concatenate([go[...], gt[...]], axis=0)
        value = mm_outer(left, right)
        for n in range(step // block):
            relative = (at * (step // block) + n) ^ where_ref[1]
            part = value[n * block : (n + 1) * block]
            for p in range(pieces):
                store_block(outs[2 * p], outs[2 * p + 1], place_of(relative, orders[p]), 0, part[:, p * 128 : (p + 1) * 128].astype(BF16))

    out = shape((devices // 2, 1, block, 128), BF16)
    return pl.pallas_call(
        body,
        grid=(tall // step,),
        in_specs=[
            S,
            pl.BlockSpec((rows, step), lambda i: (0, i)),
            pl.BlockSpec((rows, step), lambda i: (0, i)),
            pl.BlockSpec((rows, cols), lambda i: (0, 0)),
            pl.BlockSpec((rows, cols), lambda i: (0, 0)),
        ],
        out_specs=[pl.BlockSpec(out.shape, lambda i: (0, 0, 0, 0))] * (2 * pieces),
        out_shape=[out] * (2 * pieces),
        compiler_params=pltpu.CompilerParams(vmem_limit_bytes=VMEM_BYTES, fuse_transposed_lhs_in_matmul=True),
        cost_estimate=pl.CostEstimate(flops=4 * rows * tall * cols, bytes_accessed=4 * rows * (tall + cols) + 2 * tall * cols, transcendentals=0),
    )(where, x_own, x_other, g_own, g_other)


def weight_grad_wide(where, orders, parts):
    devices = 1 << len(orders[0])
    pieces = len(orders)
    rows, width = parts[0][0].shape
    block = width // devices
    blocked = [part[2].ndim == 3 for part in parts]
    tiles = [part[2].shape[0] if part[2].ndim == 3 else part[2].shape[1] // 128 for part in parts]
    subs = sum(tiles) // pieces

    def body(where_ref, *refs):
        outs = refs[4 * len(parts) :]
        sub = 0
        for n, part in enumerate(parts):
            xo, xt, go, gt = refs[4 * n : 4 * n + 4]
            left = jnp.concatenate([xo[...], xt[...]], axis=0)
            count = tiles[n] // pieces
            for p in range(pieces):
                t = 0
                while t < count:
                    two = min(2, count - t)
                    at = p * count + t
                    if blocked[n]:
                        right = jnp.concatenate(
                            [jnp.concatenate([go[at + m], gt[at + m]], axis=0) for m in range(two)], axis=1
                        )
                    else:
                        cut = pl.ds(at * 128, two * 128)
                        right = jnp.concatenate([go[:, cut], gt[:, cut]], axis=0)
                    value = mm_outer(left, right)
                    for j in range(devices):
                        relative = j ^ where_ref[1]
                        place = place_of(relative, orders[p])
                        for m in range(two):
                            part_value = value[j * block : (j + 1) * block, m * 128 : (m + 1) * 128]
                            store_block(outs[2 * p], outs[2 * p + 1], place, sub + t + m, part_value.astype(BF16))
                    t += two
            sub += count

    out = shape((devices // 2, subs, block, 128), BF16)
    args = [item for part in parts for item in part]
    return kernel_call(
        body,
        [S] + [V] * len(args),
        [out] * (2 * pieces),
        [],
        (where, *args),
        4 * rows * width * 128 * sum(tiles),
        fuse_transposed_lhs_in_matmul=True,
    )


def swap(value):
    return lax.ppermute(value, "section", [(0, 1), (1, 0)])


def across(value, bit):
    return lax.ppermute(value, "dp", [(i, i ^ (1 << bit)) for i in range(lax.axis_size("dp"))])


def scatter_sum(keep, send, order):
    for n, bit in enumerate(order):
        total = keep.astype(F32) + across(send, bit).astype(F32)
        if n + 1 < len(order):
            total = total.astype(BF16)
            half = total.shape[0] // 2
            keep, send = total[:half], total[half:]
    return total[0]


def bias_base(table, grid, rows, lanes):
    side = 2 * grid - 1
    flipped = table[: side * side].reshape(side, side, -1)[::-1, ::-1]
    base = jnp.stack([flipped[:, grid - 1 - r : 2 * grid - 1 - r] for r in range(grid)])
    base = jnp.transpose(base, (3, 0, 1, 2)).reshape(table.shape[1], grid, side * grid)
    return jnp.pad(base, ((0, 0), (0, rows - grid), (1, lanes - 1 - side * grid)))


def table_grad(folded, grid, length):
    side = 2 * grid - 1
    heads = folded.shape[0]
    body = folded[:, :grid, 1 : 1 + side * grid].reshape(heads, grid, side, grid)
    flipped = sum(
        jnp.pad(body[:, r], ((0, 0), (0, 0), (grid - 1 - r, r))) for r in range(grid)
    )
    inner = jnp.transpose(flipped[:, ::-1, ::-1], (1, 2, 0)).reshape(side * side, heads)
    first = folded[:, grid, :length]
    ends = jnp.stack([jnp.sum(first[:, 1:], axis=1), folded[:, grid + 1, 0], first[:, 0]])
    return jnp.concatenate([inner, ends], axis=0)


def body(input_big, input_small, small_counts, cotangent_big, cotangent_small, norm1_gain, norm1_bias, qkv_weight, query_bias, value_bias, table_big, table_small, proj_weight, proj_bias, attn_scale, norm2_gain, norm2_bias, up_weight, up_bias, down_weight, down_bias, mlp_scale):
    micro, crops, len_big, width = input_big.shape
    slots_all, len_small = input_small.shape[1], input_small.shape[2]
    slots = slots_all // small_counts.shape[1]
    grid_big, grid_small = math.isqrt(len_big - 1), math.isqrt(len_small - 1)
    pad_big = up_to(len_big, 16)
    real_small = slots_all * len_small
    pad_small = up_to(real_small, 16)
    split = crops * pad_big
    rows = split + pad_small
    sizes = (crops, len_big, pad_big, slots_all, len_small, pad_small)
    devices = lax.axis_size("dp")
    bits = devices.bit_length() - 1
    core = lax.axis_index("section")
    place = lax.axis_index("dp")
    where = jnp.stack([core, place]).astype(jnp.int32)
    first = core == 0

    def join(big, small):
        big = lax.dynamic_index_in_dim(big, core, 0, keepdims=False)
        small = lax.dynamic_index_in_dim(small, core, 0, keepdims=False)
        big = jnp.pad(big, ((0, 0), (0, pad_big - len_big), (0, 0))).reshape(split, width)
        small = jnp.pad(small.reshape(real_small, width), ((0, pad_small - real_small), (0, 0)))
        return jnp.concatenate([big, small])

    x0 = join(input_big, input_small)
    cotangent = join(cotangent_big, cotangent_small)
    counts = lax.dynamic_index_in_dim(small_counts, core, 0, keepdims=False)
    line = jnp.arange(rows, dtype=jnp.int32)
    spot = line - split
    limit = jnp.repeat(counts, slots * len_small, total_repeat_length=real_small)
    small_keep = (jnp.arange(real_small, dtype=jnp.int32) // len_small % slots < limit).astype(F32)
    keep = jnp.where(line < split, (line % pad_big < len_big).astype(F32), jnp.pad(small_keep, (split, pad_small - real_small)))
    keep = keep[:, None]

    vec_own = jnp.concatenate(
        [norm1_gain, norm1_bias, query_bias, value_bias, proj_bias, attn_scale, norm2_gain, norm2_bias, down_bias, mlp_scale, up_bias.reshape(-1, width)]
    )
    tables_own = jnp.concatenate([table_big[0], table_small[0]])
    vec_other, tables_other = swap(vec_own), swap(tables_own)
    qkv = (qkv_weight[0], swap(qkv_weight[0]))
    proj = (proj_weight[0], swap(proj_weight[0]))
    up = (up_weight[0], swap(up_weight[0]))
    down = (down_weight[0], swap(down_weight[0]))

    layers = []
    for layer in range(2):
        vec = jnp.where(core == layer, vec_own, vec_other)
        tables = jnp.where(core == layer, tables_own, tables_other)
        part_big, part_small = tables[: table_big.shape[1]], tables[table_big.shape[1] :]
        ups = vec[10:].reshape(1, -1)
        joined = jnp.concatenate([vec[2:3], jnp.zeros_like(vec[2:3]), vec[3:4]], axis=1)
        corners = jnp.stack([part_big[-3:], part_small[-3:]])
        base_big = bias_base(part_big, grid_big, 16, 512)
        base_small = bias_base(part_small, grid_small, 8, 256)
        layers.append((vec, ups, joined, corners, base_big, base_small))

    saved = []
    x = x0
    outs = []
    for layer in range(2):
        vec, ups, joined, corners, base_big, base_small = layers[layer]
        normed, projected = qkv_forward(layer, where, x, vec[0:1], vec[1:2], joined, *qkv)
        attended = attention_forward(projected, base_big, base_small, corners, sizes)
        branch, middle, normed2, hidden, slope = up_forward(layer, where, attended, x, vec, ups, *proj, *up)
        y, mlp = down_forward(layer, where, hidden, middle, keep, vec, *down)
        saved.append((x, normed, projected, attended, branch, middle, normed2, hidden, slope, mlp))
        outs.append(y)
        x = y

    orders = [list(range(bits)), [1, 0] + list(range(2, bits)), [2, 0, 1] + list(range(3, bits))]
    g = cotangent
    backs = [None, None]
    sums = [None, None]
    flats = [None, None]
    for layer in (1, 0):
        vec, ups, joined, corners, base_big, base_small = layers[layer]
        x, normed, projected, attended, branch, middle, normed2, hidden, slope, mlp = saved[layer]
        hidden_other, normed2_other, attended_other, normed_other = swap(hidden), swap(normed2), swap(attended), swap(normed)
        gm, gp, gb, ga, gmid, vecs2, up_sum = mlp_backward(layer, where, g, keep, vec, slope, middle, branch, down, up, proj)
        scale_sum = jnp.sum(g.astype(F32) * keep * mlp, axis=0, keepdims=True)
        gm_other, gp_other, gb_other = swap(gm[1]), swap(gp[1]), swap(gb[1])
        tall = weight_grad_tall(where, orders, hidden, hidden_other, gm[0], gm_other)
        wide = weight_grad_wide(where, orders, [(normed2, normed2_other, gp[0], gp_other)])
        gproj, fold_big, fold_small, qv_sum = attention_backward(where, projected, ga, base_big, base_small, corners, sizes)
        half = gproj.shape[0] // 2
        gproj_other = swap(gproj[half:])
        g, vecs1 = qkv_backward(layer, where, gproj, x, gmid, vec[0:1], *qkv)
        last = weight_grad_wide(where, orders, [(attended, attended_other, gb[0], gb_other), (normed, normed_other, gproj[:half], gproj_other)])
        backs[layer] = g
        sums[layer] = [
            scatter_sum(group[2 * p], group[2 * p + 1], orders[p]) for group in (tall, wide, last) for p in range(3)
        ]
        small = jnp.concatenate([vecs1, qv_sum, vecs2[3:4], vecs2[2:3], vecs2[0:2], vecs2[4:5], scale_sum, up_sum.reshape(-1, width)])
        flat = jnp.concatenate(
            [small.reshape(-1), table_grad(fold_big, grid_big, len_big).reshape(-1), table_grad(fold_small, grid_small, len_small).reshape(-1)]
        )
        flat = jnp.pad(flat, (0, up_to(flat.shape[0], 1024) - flat.shape[0])).reshape(-1, 128)
        flat = flat + swap(flat)
        for bit in range(bits):
            flat = flat + across(flat, bit)
        flats[layer] = flat.reshape(-1)

    def pick(zero, one):
        return jnp.where(first, zero, one)

    def unpad(value):
        big = value[:split].reshape(crops, pad_big, width)[:, :len_big]
        return big, value[split : split + real_small].reshape(slots_all, len_small, width)

    def assemble(zero, one):
        kept, came = pick(zero, one), swap(pick(one, zero))
        parts = [pick(kept, came), pick(came, kept)]
        pairs = [unpad(part) for part in parts]
        return jnp.stack([p[0] for p in pairs])[None], jnp.stack([p[1] for p in pairs])[None]

    layer_big, layer_small = assemble(*outs)
    grad_big, grad_small = assemble(*backs)

    block = width // devices
    halves = [[], []]
    for zero, one in zip(sums[0], sums[1]):
        kept, came = pick(zero, one), swap(pick(one, zero))
        halves[0].append(pick(kept, came))
        halves[1].append(pick(came, kept))

    def columns(pieces, low, high):
        tiles = [piece[n] for piece in pieces for n in range(low, high)]
        return jnp.concatenate(tiles, axis=1)

    grad_down = jnp.concatenate([columns(side[0:3], 0, 1) for side in halves], axis=1)
    wide_subs = sums[0][3].shape[0]
    grad_up = jnp.concatenate([columns(side[3:6], 0, wide_subs) for side in halves], axis=1)
    grad_proj = jnp.concatenate([columns(side[6:9], 0, 1) for side in halves], axis=1)
    grad_qkv = jnp.concatenate([columns(side[6:9], 1, wide_subs) for side in halves], axis=1)

    flat = pick(flats[0], flats[1])

    def vector(row, count=1):
        whole = flat[row * width : (row + count) * width]
        size = count * block
        return lax.dynamic_slice_in_dim(whole, place * size, size)[None]

    ff = up_bias.shape[1] // width
    start = (10 + ff) * width
    size_big, size_small = table_big.shape[1] * HEADS, table_small.shape[1] * HEADS
    grad_table_big = flat[start : start + size_big].reshape(table_big.shape)
    grad_table_small = flat[start + size_big : start + size_big + size_small].reshape(table_small.shape)
    return (
        layer_big,
        layer_small,
        grad_big,
        grad_small,
        vector(0),
        vector(1),
        grad_qkv[None],
        vector(2),
        vector(3),
        grad_table_big,
        grad_table_small,
        grad_proj[None],
        vector(4),
        vector(5),
        vector(6),
        vector(7),
        grad_up[None],
        vector(10, ff),
        grad_down[None],
        vector(8),
        vector(9),
    )


def solution(mesh):
    row = P("section", None)
    whole = P("section", None, None)
    dp4 = P(None, "dp", None, None)
    in_specs = (dp4, dp4, P(None, "dp"), dp4, dp4, row, row, whole, row, row, whole, whole, whole, row, row, row, row, whole, row, whole, row, row)
    out5 = P("section", None, "dp", None, None)
    vec = P("section", "dp")
    mat = P("section", "dp", None)
    out_specs = (out5, out5, out5, out5, vec, vec, mat, vec, vec, whole, whole, mat, vec, vec, vec, vec, mat, vec, mat, vec, vec)
    return jax.shard_map(body, mesh=mesh, in_specs=in_specs, out_specs=out_specs, check_vma=False)
```

time: 2430 us -> 793 us (0.33)
  other arithmetic: 779 us -> 33.7 us
  local copies, waits for them, and re-layouts: 640 us -> 178 us
  waiting for transfers between devices: 562 us -> 158 us
  matrix products: 403 us -> 0 us
  Pallas kernels: 0 us -> 310 us
  starting transfers between devices: 9.12 us -> 100 us
    scatter-add x6 -> x0, other arithmetic: 635 us -> none  [attend_backward(): jax.ops.segment_sum(summed.T, index.reshape(-1), num_segments=table.shape...]
    reduce_scatter x4 -> x0, waiting for transfers between devices: 561 us -> none  [the longest x1 177 us: body(): lax.psum_scatter(pending[10], 'dp', scatter_dimension=0, tiled=True)]
    dot_general x96 -> x0, matrix products: 403 us -> none  [the longest x12 76.2 us: outer_sum(): lax.dot_general(left, right, (((0,), (0,)), ((), ())), preferred_element_...]
    pallas_call x0 -> x20, Pallas kernels: none -> 310 us  [the longest x14 208 us: kernel_call(): pl.pallas_call(body, in_specs=ins, out_specs=[V] * len(outs), out_shape=o...]
    gather x6 -> x0, local copies, waits for them, and re-layouts: 167 us -> none  [score_block(): bias = jnp.transpose(jnp.take(table, index, axis=0), (2, 0, 1))]
    ppermute x4 -> x115, waiting for transfers between devices: 1.24 us -> 158 us  [the longest x80 150 us: across(): lax.ppermute(value, 'dp', [(i, i ^ 1 << bit) for i in range(lax.axis_size...]
    ppermute x4 -> x115, starting transfers between devices: 8.3 us -> 100 us  [the longest x80 93.4 us: across(): lax.ppermute(value, 'dp', [(i, i ^ 1 << bit) for i in range(lax.axis_size...]
    reshape x37, local copies, waits for them, and re-layouts: 95.5 us -> 20.3 us  [the longest x4 8.6 us: table_grad(): body = folded[:, :grid, 1:1 + side * grid].reshape(heads, grid, side, grid)]
  transfers between devices with their start and end apart: 9 -> 115, of which waited for: 5 -> 69; matrix products, arithmetic and copies ran while one was open for 30% -> 26% of each run, Pallas kernels for 0% -> 36%
where the time goes in v1:
time: 793 us; the launch traced here: 783 us
  Pallas kernels  310 us (39%)
  local copies, waits for them, and re-layouts  178 us (22%)
  waiting for transfers between devices  158 us (20%)
  starting transfers between devices  100 us (13%)
  other arithmetic  33.7 us (4%)
    pallas_call x14, Pallas kernels, kernel_call(): pl.pallas_call(body, in_specs=ins, out_specs=[V] * len(outs), out_shape=o...  208 us
    ppermute x80, waiting for transfers between devices, across(): lax.ppermute(value, 'dp', [(i, i ^ 1 << bit) for i in range(lax.axis_size...  150 us
    ppermute x80, starting transfers between devices, across(): lax.ppermute(value, 'dp', [(i, i ^ 1 << bit) for i in range(lax.axis_size...  93.4 us
    pallas_call x2, Pallas kernels, attention_backward(): pl.pallas_call(clear, grid=(pairs,), in_specs=[S, S, pl.BlockSpec((rows,...  50.2 us
    slice x44, local copies, waits for them, and re-layouts, bias_base(): flipped[:, grid - 1 - r:2 * grid - 1 - r]  46 us
    unnamed x319, local copies, waits for them, and re-layouts  44.5 us
    pallas_call x2, Pallas kernels, attention_forward(): pl.pallas_call(body, grid=(pairs,), in_specs=[S, pl.BlockSpec((rows, 128)...  27.1 us
    pallas_call x2, Pallas kernels, weight_grad_tall(): pl.pallas_call(body, grid=(tall // step,), in_specs=[S, pl.BlockSpec((row...  24.6 us
  transfers between devices with their start and end apart: 115, of which 69 were waited for; matrix products, arithmetic and copies ran while one was open for 26% of the time, Pallas kernels for 36%

profile of v1, /device:TPU:0, one launch (start us, length us, event | category | flops | bytes accessed | tf_op | source)
XLA Modules:
  0.0 783.4 jit_solution(6367045999584961055)
XLA Ops:
  119.7 7.0 shard_map.373
  126.7 13.8 %shard_map.374.att_ref.refs_0_ = bf16[576,768]{1,0:T(8,128)(2,1)} custom-call(f32[2,3,12]{2,1,0:T(4,128)} %pad_maximum_fusion.7.corner_ref.refs_1_, bf16[576,2304]{1,0:T(8,128)(2,1)} %get-tuple-element.125.q_ref.k_ref.v_ref.refs_2_.refs_3_.refs_4_, bf16[576,2304]{1,0:T(8,128)(2,1)} %get-tuple-element.125.q_ref.k_ref.v_ref.refs_2_.refs_3_.refs_4_, ...), custom_call_target="tpu_custom_call" | custom-call | flops 8000000000 | bytes 3538944 | tf_op jit(solution)/shard_map/pallas_call | solution.py:195
  141.5 17.3 %shard_map.375 = (f32[576,768]{1,0:T(8,128)}, f32[576,768]{1,0:T(8,128)}, bf16[576,768]{1,0:T(8,128)(2,1)}, bf16[576,3072]{1,0:T(8,128)(2,1)}, bf16[576,3072]{1,0:T(8,128)(2,1)}) custom-call(s32[2]{0:T(128)} %pad_add_fusion.4.core_ref.refs_0_.where_ref, bf16[576,768]{1,0:T(8,128)(2,1)} %shard_map.374.att_ref.refs_0_, bf16[576,768]{1,0:T(8,128)(2,1)} %fusion.2.x_ref, ...), custom_call_target="tpu_custom_call" | custom-call | flops 3397386240 | bytes 25122824 | tf_op jit(solution)/shard_map/pallas_call | solution.py:99
  158.9 9.6 %shard_map.376 = (bf16[576,768]{1,0:T(8,128)(2,1)}, f32[576,768]{1,0:T(8,128)}) custom-call(s32[2]{0:T(128)} %pad_add_fusion.4.core_ref.refs_0_.where_ref, bf16[576,3072]{1,0:T(8,128)(2,1)} %get-tuple-element.126.hidden_ref.xo, f32[576,768]{1,0:T(8,128)} %get-tuple-element.127.middle_ref, f32[576,1]{1,0:T(8,128)} %broadcast_in_dim.94.keep_ref, ...), custom_call_target="tpu_custom_call" | custom-call | flops 2717908992 | bytes 17445128 | tf_op jit(solution)/shard_map/pallas_call | solution.py:99
  168.5 7.0 shard_map.377
  175.5 13.4 %shard_map.378.att_ref.refs_0_ = bf16[576,768]{1,0:T(8,128)(2,1)} custom-call(f32[2,3,12]{2,1,0:T(4,128)} %pad_maximum_fusion.8.corner_ref.refs_1_, bf16[576,2304]{1,0:T(8,128)(2,1)} %get-tuple-element.129.q_ref.k_ref.v_ref.refs_2_.refs_3_.refs_4_, bf16[576,2304]{1,0:T(8,128)(2,1)} %get-tuple-element.129.q_ref.k_ref.v_ref.refs_2_.refs_3_.refs_4_, ...), custom_call_target="tpu_custom_call" | custom-call | flops 8000000000 | bytes 3538944 | tf_op jit(solution)/shard_map/pallas_call | solution.py:195
  189.3 17.3 %shard_map.379 = (f32[576,768]{1,0:T(8,128)}, f32[576,768]{1,0:T(8,128)}, bf16[576,768]{1,0:T(8,128)(2,1)}, bf16[576,3072]{1,0:T(8,128)(2,1)}, bf16[576,3072]{1,0:T(8,128)(2,1)}) custom-call(s32[2]{0:T(128)} %pad_add_fusion.4.core_ref.refs_0_.where_ref, bf16[576,768]{1,0:T(8,128)(2,1)} %shard_map.378.att_ref.refs_0_, ...), custom_call_target="tpu_custom_call" | custom-call | flops 3397386240 | bytes 25122824 | tf_op jit(solution)/shard_map/pallas_call | solution.py:99
  206.6 19.6 %shard_map.381 = (bf16[2,576,384]{2,1,0:T(8,128)(2,1)}, bf16[2,576,1536]{2,1,0:T(8,128)(2,1)}, bf16[2,576,384]{2,1,0:T(8,128)(2,1)}, bf16[576,768]{1,0:T(8,128)(...) custom-call(s32[2]{0:T(128)} %pad_add_fusion.4.core_ref.refs_0_.where_ref, ...), custom_call_target="tpu_custom_call" | custom-call | flops 6115295232 | bytes 37241096 | tf_op jit(solution)/shard_map/pallas_call | solution.py:99
  226.1 24.9 %shard_map.382 = (bf16[18,576,128]{2,1,0:T(8,128)(2,1)}, f32[12,16,512]{2,1,0:T(8,128)}, f32[12,8,256]{2,1,0:T(8,128)}, f32[2,768]{1,0:T(2,128)}) custom-call(s32[2]{0:T(128)} %pad_add_fusion.4.core_ref.refs_0_.where_ref, f32[2,3,12]{2,1,0:T(4,128)} %pad_maximum_fusion.8.corner_ref.refs_1_, ...), custom_call_target="tpu_custom_call" | custom-call | flops 20000000000 | bytes 7077888 | tf_op jit(solution)/shard_map/pallas_call | solution.py:460
  254.4 9.0 %shard_map.383 = (bf16[576,768]{1,0:T(8,128)(2,1)}, f32[2,768]{1,0:T(2,128)}) custom-call(s32[2]{0:T(128)} %pad_add_fusion.4.core_ref.refs_0_.where_ref, bf16[18,576,128]{2,1,0:T(8,128)(2,1)} %get-tuple-element.136.gproj_ref, bf16[576,768]{1,0:T(8,128)(2,1)} %get-tuple-element.128.x_ref, f32[576,768]{1,0:T(8,128)} %get-tuple-element.137.gmid_ref, ...), custom_call_target="tpu_custom_call" | custom-call | flops 2038431744 | bytes 13280264 | tf_op jit(solution)/shard_map/pallas_call | solution.py:99
  263.4 19.0 %shard_map.384 = (bf16[2,576,384]{2,1,0:T(8,128)(2,1)}, bf16[2,576,1536]{2,1,0:T(8,128)(2,1)}, bf16[2,576,384]{2,1,0:T(8,128)(2,1)}, bf16[576,768]{1,0:T(8,128)(...) custom-call(s32[2]{0:T(128)} %pad_add_fusion.4.core_ref.refs_0_.where_ref, ...), custom_call_target="tpu_custom_call" | custom-call | flops 6115295232 | bytes 37241096 | tf_op jit(solution)/shard_map/pallas_call | solution.py:99
  282.5 25.3 %shard_map.385 = (bf16[18,576,128]{2,1,0:T(8,128)(2,1)}, f32[12,16,512]{2,1,0:T(8,128)}, f32[12,8,256]{2,1,0:T(8,128)}, f32[2,768]{1,0:T(2,128)}) custom-call(s32[2]{0:T(128)} %pad_add_fusion.4.core_ref.refs_0_.where_ref, f32[2,3,12]{2,1,0:T(4,128)} %pad_maximum_fusion.7.corner_ref.refs_1_, ...), custom_call_target="tpu_custom_call" | custom-call | flops 20000000000 | bytes 7077888 | tf_op jit(solution)/shard_map/pallas_call | solution.py:460
  332.8 9.8 %shard_map.380 = (bf16[576,768]{1,0:T(8,128)(2,1)}, f32[576,768]{1,0:T(8,128)}) custom-call(s32[2]{0:T(128)} %pad_add_fusion.4.core_ref.refs_0_.where_ref, bf16[576,3072]{1,0:T(8,128)(2,1)} %get-tuple-element.130.hidden_ref.xo, f32[576,768]{1,0:T(8,128)} %get-tuple-element.131.middle_ref, f32[576,1]{1,0:T(8,128)} %broadcast_in_dim.94.keep_ref, ...), custom_call_target="tpu_custom_call" | custom-call | flops 2717908992 | bytes 17445128 | tf_op jit(solution)/shard_map/pallas_call | solution.py:99
  345.3 9.0 %shard_map.386 = (bf16[576,768]{1,0:T(8,128)(2,1)}, f32[2,768]{1,0:T(2,128)}) custom-call(s32[2]{0:T(128)} %pad_add_fusion.4.core_ref.refs_0_.where_ref, bf16[18,576,128]{2,1,0:T(8,128)(2,1)} %get-tuple-element.142.gproj_ref, bf16[576,768]{1,0:T(8,128)(2,1)} %fusion.2.x_ref, f32[576,768]{1,0:T(8,128)} %get-tuple-element.143.gmid_ref, ...), custom_call_target="tpu_custom_call" | custom-call | flops 2038431744 | bytes 13280264 | tf_op jit(solution)/shard_map/pallas_call | solution.py:99
  424.9 22.9 %shard_map.388 = (bf16[8,4,48,128]{3,2,1,0:T(8,128)(2,1)}, bf16[8,4,48,128]{3,2,1,0:T(8,128)(2,1)}, bf16[8,4,48,128]{3,2,1,0:T(8,128)(2,1)}, bf16[8,4,48,128]{3,...) custom-call(s32[2]{0:T(128)} %pad_add_fusion.4.core_ref.refs_0_.where_ref, ...), custom_call_target="tpu_custom_call" | custom-call | flops 2717908992 | bytes 9437192 | tf_op jit(solution)/shard_map/pallas_call | solution.py:99
  448.8 23.2 %shard_map.387 = (bf16[8,4,48,128]{3,2,1,0:T(8,128)(2,1)}, bf16[8,4,48,128]{3,2,1,0:T(8,128)(2,1)}, bf16[8,4,48,128]{3,2,1,0:T(8,128)(2,1)}, bf16[8,4,48,128]{3,...) custom-call(s32[2]{0:T(128)} %pad_add_fusion.4.core_ref.refs_0_.where_ref, ...), custom_call_target="tpu_custom_call" | custom-call | flops 2717908992 | bytes 9437192 | tf_op jit(solution)/shard_map/pallas_call | solution.py:99
  489.1 7.1 collective-permute-done.35
  510.0 18.5 %shard_map.390 = (bf16[8,4,48,128]{3,2,1,0:T(8,128)(2,1)}, bf16[8,4,48,128]{3,2,1,0:T(8,128)(2,1)}, bf16[8,4,48,128]{3,2,1,0:T(8,128)(2,1)}, bf16[8,4,48,128]{3,...) custom-call(s32[2]{0:T(128)} %pad_add_fusion.4.core_ref.refs_0_.where_ref, ...), custom_call_target="tpu_custom_call" | custom-call | flops 2717908992 | bytes 7667720 | tf_op jit(solution)/shard_map/pallas_call | solution.py:99
  530.6 18.6 %shard_map.389 = (bf16[8,4,48,128]{3,2,1,0:T(8,128)(2,1)}, bf16[8,4,48,128]{3,2,1,0:T(8,128)(2,1)}, bf16[8,4,48,128]{3,2,1,0:T(8,128)(2,1)}, bf16[8,4,48,128]{3,...) custom-call(s32[2]{0:T(128)} %pad_add_fusion.4.core_ref.refs_0_.where_ref, ...), custom_call_target="tpu_custom_call" | custom-call | flops 2717908992 | bytes 7667720 | tf_op jit(solution)/shard_map/pallas_call | solution.py:99
  607.8 6.7 collective-permute-done.75
  617.8 7.5 collective-permute-done.66
  628.3 9.0 %collective-permute-done.55 = bf16[8,4,48,128]{3,2,1,0:T(8,128)(2,1)S(1)} collective-permute-done((bf16[8,4,48,128]{3,2,1,0:T(8,128)(2,1)S(1)}, bf16[8,4,48,128]{3,2,1,0:T(8,128)(2,1)S(1)}, u32[]{:S(2)}, u32[]{:S(2)}) %collective-permute-start.55) | collective-permute-done | bytes 393248 | tf_op jit(solution)/shard_map/ppermute | solution.py:649
  696.9 12.4 %shard_map.392 = (bf16[8,1,192,128]{3,2,1,0:T(8,128)(2,1)}, bf16[8,1,192,128]{3,2,1,0:T(8,128)(2,1)}, bf16[8,1,192,128]{3,2,1,0:T(8,128)(2,1)}, bf16[8,1,192,128...) custom-call(s32[2]{0:T(128)} %pad_add_fusion.4.core_ref.refs_0_.where_ref, ...), custom_call_target="tpu_custom_call" | custom-call | flops 2717908992 | bytes 10321920 | tf_op jit(solution)/shard_map/pallas_call | solution.py:576
  709.4 12.2 %shard_map.391 = (bf16[8,1,192,128]{3,2,1,0:T(8,128)(2,1)}, bf16[8,1,192,128]{3,2,1,0:T(8,128)(2,1)}, bf16[8,1,192,128]{3,2,1,0:T(8,128)(2,1)}, bf16[8,1,192,128...) custom-call(s32[2]{0:T(128)} %pad_add_fusion.4.core_ref.refs_0_.where_ref, ...), custom_call_target="tpu_custom_call" | custom-call | flops 2717908992 | bytes 10321920 | tf_op jit(solution)/shard_map/pallas_call | solution.py:576
  (923 shorter events, 439.6 us)
Async XLA Ops:
  7.5 108.9 %collective-permute-start.1 = (f32[14,768]{1,0:T(8,128)}, f32[14,768]{1,0:T(8,128)}, u32[]{:S(2)}, u32[]{:S(2)}) collective-permute-start(f32[14,768]{1,0:T(8,128)} %concatenate.60), channel_id=1, source_target_pairs={{0,16},{16,0},{1,17},{17,1},{2,18},{18,2},{3,19},{19,3},{4,20},{20... | collective-permute-start | bytes 129032 | tf_op jit(solution)/shard_map/ppermute | solution.py:645
  7.5 112.2 %collective-permute-start.2 = (bf16[768,2304]{1,0:T(8,128)(2,1)}, bf16[768,2304]{1,0:T(8,128)(2,1)}, u32[]{:S(2)}, u32[]{:S(2)}) collective-permute-start(bf16[768,2304]{1,0:T(8,128)(2,1)} %bitcast.722), channel_id=1, source_target_pairs={{0,16},{16,0},{1,17},{17,1},{2,18},{18,2},{3,19},{19,3},{4,20},{20... | collective-permute-start | bytes 10616840 | tf_op jit(solution)/shard_map/ppermute | solution.py:645
  8.0 132.6 %collective-permute-start.4 = (bf16[768,3072]{1,0:T(8,128)(2,1)}, bf16[768,3072]{1,0:T(8,128)(2,1)}, u32[]{:S(2)}, u32[]{:S(2)}) collective-permute-start(bf16[768,3072]{1,0:T(8,128)(2,1)} %bitcast.712), channel_id=1, source_target_pairs={{0,16},{16,0},{1,17},{17,1},{2,18},{18,2},{3,19},{19,3},{4,20},{20... | collective-permute-start | bytes 14155784 | tf_op jit(solution)/shard_map/ppermute | solution.py:645
  8.0 132.5 %collective-permute-start.3 = (bf16[768,768]{1,0:T(8,128)(2,1)}, bf16[768,768]{1,0:T(8,128)(2,1)S(1)}, u32[]{:S(2)}, u32[]{:S(2)}) collective-permute-start(bf16[768,768]{1,0:T(8,128)(2,1)} %bitcast.727), channel_id=1, source_target_pairs={{0,16},{16,0},{1,17},{17,1},{2,18},{18,2},{3,19},{19,3},{4,20},{20... | collective-permute-start | bytes 3538952 | tf_op jit(solution)/shard_map/ppermute | solution.py:645
  17.7 141.2 %collective-permute-start.5 = (bf16[3072,768]{1,0:T(8,128)(2,1)}, bf16[3072,768]{1,0:T(8,128)(2,1)}, u32[]{:S(2)}, u32[]{:S(2)}) collective-permute-start(bf16[3072,768]{1,0:T(8,128)(2,1)} %bitcast.717), channel_id=1, source_target_pairs={{0,16},{16,0},{1,17},{17,1},{2,18},{18,2},{3,19},{19,3},{4,20},{20... | collective-permute-start | bytes 14155784 | tf_op jit(solution)/shard_map/ppermute | solution.py:645
  188.8 221.4 %collective-permute-start.26 = (bf16[576,768]{1,0:T(8,128)(2,1)}, bf16[576,768]{1,0:T(8,128)(2,1)}, u32[]{:S(2)}, u32[]{:S(2)}) collective-permute-start(bf16[576,768]{1,0:T(8,128)(2,1)} %shard_map.378.att_ref.refs_0_), channel_id=1, source_target_pairs={{0,16},{16,0},{1,17},{17,1},{2,18},{18,2},{3,19},{19,3},{4,20},{20... | collective-permute-start | bytes 2654216 | tf_op jit(solution)/shard_map/ppermute | solution.py:645
  321.3 103.3 %collective-permute-start.29 = (bf16[9,576,128]{2,1,0:T(8,128)(2,1)}, bf16[9,576,128]{2,1,0:T(8,128)(2,1)}, u32[]{:S(2)}, u32[]{:S(2)}) collective-permute-start(bf16[9,576,128]{2,1,0:T(8,128)(2,1)} %get-tuple-element.302), channel_id=1, source_target_pairs={{0,16},{16,0},{1,17},{17,1},{2,18},{18,2},{3,19},{19,3},{4,20},{20... | collective-permute-start | bytes 3981320 | tf_op jit(solution)/shard_map/ppermute | solution.py:645
  385.7 19.9 %collective-permute-start.27 = (bf16[576,384]{1,0:T(8,128)(2,1)}, bf16[576,384]{1,0:T(8,128)(2,1)}, u32[]{:S(2)}, u32[]{:S(2)}) collective-permute-start(bf16[576,384]{1,0:T(8,128)(2,1)} %get-tuple-element.314), channel_id=1, source_target_pairs={{0,16},{16,0},{1,17},{17,1},{2,18},{18,2},{3,19},{19,3},{4,20},{20... | collective-permute-start | bytes 1327112 | tf_op jit(solution)/shard_map/ppermute | solution.py:645
  406.1 42.0 %collective-permute-start.21 = (bf16[9,576,128]{2,1,0:T(8,128)(2,1)}, bf16[9,576,128]{2,1,0:T(8,128)(2,1)}, u32[]{:S(2)}, u32[]{:S(2)}) collective-permute-start(bf16[9,576,128]{2,1,0:T(8,128)(2,1)} %get-tuple-element.304), channel_id=1, source_target_pairs={{0,16},{16,0},{1,17},{17,1},{2,18},{18,2},{3,19},{19,3},{4,20},{20... | collective-permute-start | bytes 3981320 | tf_op jit(solution)/shard_map/ppermute | solution.py:645
  410.3 37.6 %collective-permute-start.18 = (bf16[576,768]{1,0:T(8,128)(2,1)}, bf16[576,768]{1,0:T(8,128)(2,1)}, u32[]{:S(2)}, u32[]{:S(2)}) collective-permute-start(bf16[576,768]{1,0:T(8,128)(2,1)} %shard_map.374.att_ref.refs_0_), channel_id=1, source_target_pairs={{0,16},{16,0},{1,17},{17,1},{2,18},{18,2},{3,19},{19,3},{4,20},{20... | collective-permute-start | bytes 2654216 | tf_op jit(solution)/shard_map/ppermute | solution.py:645
  410.4 37.6 %collective-permute-start.20 = (bf16[576,768]{1,0:T(8,128)(2,1)}, bf16[576,768]{1,0:T(8,128)(2,1)}, u32[]{:S(2)}, u32[]{:S(2)}) collective-permute-start(bf16[576,768]{1,0:T(8,128)(2,1)} %get-tuple-element.160.refs_4_), channel_id=1, source_target_pairs={{0,16},{16,0},{1,17},{17,1},{2,18},{18,2},{3,19},{19,3},{4,20},{20... | collective-permute-start | bytes 2654216 | tf_op jit(solution)/shard_map/ppermute | solution.py:645
  421.5 26.5 %collective-permute-start.19 = (bf16[576,384]{1,0:T(8,128)(2,1)S(1)}, bf16[576,384]{1,0:T(8,128)(2,1)S(1)}, u32[]{:S(2)}, u32[]{:S(2)}) collective-permute-start(bf16[576,384]{1,0:T(8,128)(2,1)S(1)} %copy-done.49), channel_id=1, source_target_pairs={{0,16},{16,0},{1,17},{17,1},{2,18},{18,2},{3,19},{19,3},{4,20},{20... | collective-permute-start | bytes 1327112 | tf_op jit(solution)/shard_map/ppermute | solution.py:645
  424.5 84.6 %collective-permute-start.60 = (bf16[576,1536]{1,0:T(8,128)(2,1)}, bf16[576,1536]{1,0:T(8,128)(2,1)}, u32[]{:S(2)}, u32[]{:S(2)}) collective-permute-start(bf16[576,1536]{1,0:T(8,128)(2,1)} %get-tuple-element.270), channel_id=1, source_target_pairs={{0,16},{16,0},{1,17},{17,1},{2,18},{18,2},{3,19},{19,3},{4,20},{20... | collective-permute-start | bytes 5308424 | tf_op jit(solution)/shard_map/ppermute | solution.py:645
  447.8 82.2 %collective-permute-start.54 = (bf16[576,1536]{1,0:T(8,128)(2,1)}, bf16[576,1536]{1,0:T(8,128)(2,1)}, u32[]{:S(2)}, u32[]{:S(2)}) collective-permute-start(bf16[576,1536]{1,0:T(8,128)(2,1)} %get-tuple-element.272), channel_id=1, source_target_pairs={{0,16},{16,0},{1,17},{17,1},{2,18},{18,2},{3,19},{19,3},{4,20},{20... | collective-permute-start | bytes 5308424 | tf_op jit(solution)/shard_map/ppermute | solution.py:645
  448.0 30.4 %collective-permute-start.48 = (bf16[8,4,48,128]{3,2,1,0:T(8,128)(2,1)}, bf16[8,4,48,128]{3,2,1,0:T(8,128)(2,1)S(1)}, u32[]{:S(2)}, u32[]{:S(2)}) collective-permute-start(bf16[8,4,48,128]{3,2,1,0:T(8,128)(2,1)} %get-tuple-element.174), channel_id=1, source_target_pairs={{0,4},{1,5},{2,6},{3,7},{4,0},{5,1},{6,2},{7,3},{8,12},{9,13},{10,... | collective-permute-start | bytes 1179656 | tf_op jit(solution)/shard_map/ppermute | solution.py:649
  488.9 19.6 %collective-permute-start.59 = (bf16[576,768]{1,0:T(8,128)(2,1)S(1)}, bf16[576,768]{1,0:T(8,128)(2,1)S(1)}, u32[]{:S(2)}, u32[]{:S(2)}) collective-permute-start(bf16[576,768]{1,0:T(8,128)(2,1)S(1)} %copy-done.95), channel_id=1, source_target_pairs={{0,16},{16,0},{1,17},{17,1},{2,18},{18,2},{3,19},{19,3},{4,20},{20... | collective-permute-start | bytes 2654216 | tf_op jit(solution)/shard_map/ppermute | solution.py:645
  496.1 32.4 %collective-permute-start.53 = (bf16[576,768]{1,0:T(8,128)(2,1)}, bf16[576,768]{1,0:T(8,128)(2,1)}, u32[]{:S(2)}, u32[]{:S(2)}) collective-permute-start(bf16[576,768]{1,0:T(8,128)(2,1)} %get-tuple-element.175.refs_0_), channel_id=1, source_target_pairs={{0,16},{16,0},{1,17},{17,1},{2,18},{18,2},{3,19},{19,3},{4,20},{20... | collective-permute-start | bytes 2654216 | tf_op jit(solution)/shard_map/ppermute | solution.py:645
  507.7 188.5 %collective-permute-start.90 = (bf16[576,3072]{1,0:T(8,128)(2,1)S(1)}, bf16[576,3072]{1,0:T(8,128)(2,1)}, u32[]{:S(2)}, u32[]{:S(2)}) collective-permute-start(bf16[576,3072]{1,0:T(8,128)(2,1)S(1)} %copy-done.10), channel_id=1, source_target_pairs={{0,16},{16,0},{1,17},{17,1},{2,18},{18,2},{3,19},{19,3},{4,20},{20... | collective-permute-start | bytes 10616840 | tf_op jit(solution)/shard_map/ppermute | solution.py:645
  508.6 200.8 %collective-permute-start.84 = (bf16[576,3072]{1,0:T(8,128)(2,1)S(1)}, bf16[576,3072]{1,0:T(8,128)(2,1)}, u32[]{:S(2)}, u32[]{:S(2)}) collective-permute-start(bf16[576,3072]{1,0:T(8,128)(2,1)S(1)} %copy-done.9), channel_id=1, source_target_pairs={{0,16},{16,0},{1,17},{17,1},{2,18},{18,2},{3,19},{19,3},{4,20},{20... | collective-permute-start | bytes 10616840 | tf_op jit(solution)/shard_map/ppermute | solution.py:645
  509.5 186.6 %collective-permute-start.91 = (bf16[576,384]{1,0:T(8,128)(2,1)}, bf16[576,384]{1,0:T(8,128)(2,1)}, u32[]{:S(2)}, u32[]{:S(2)}) collective-permute-start(bf16[576,384]{1,0:T(8,128)(2,1)} %get-tuple-element.310), channel_id=1, source_target_pairs={{0,16},{16,0},{1,17},{17,1},{2,18},{18,2},{3,19},{19,3},{4,20},{20... | collective-permute-start | bytes 1327112 | tf_op jit(solution)/shard_map/ppermute | solution.py:645
  528.5 20.7 %collective-permute-start.49 = (bf16[4,4,48,128]{3,2,1,0:T(8,128)(2,1)}, bf16[4,4,48,128]{3,2,1,0:T(8,128)(2,1)}, u32[]{:S(2)}, u32[]{:S(2)}) collective-permute-start(bf16[4,4,48,128]{3,2,1,0:T(8,128)(2,1)} %slice.1689), channel_id=1, source_target_pairs={{0,1},{1,0},{2,3},{3,2},{4,5},{5,4},{6,7},{7,6},{8,9},{9,8},{10,11... | collective-permute-start | bytes 589832 | tf_op jit(solution)/shard_map/ppermute | solution.py:649
  530.0 21.7 %collective-permute-start.45 = (bf16[4,4,48,128]{3,2,1,0:T(8,128)(2,1)}, bf16[4,4,48,128]{3,2,1,0:T(8,128)(2,1)}, u32[]{:S(2)}, u32[]{:S(2)}) collective-permute-start(bf16[4,4,48,128]{3,2,1,0:T(8,128)(2,1)} %slice.1683), channel_id=1, source_target_pairs={{0,1},{1,0},{2,3},{3,2},{4,5},{5,4},{6,7},{7,6},{8,9},{9,8},{10,11... | collective-permute-start | bytes 589832 | tf_op jit(solution)/shard_map/ppermute | solution.py:649
  689.5 19.9 %collective-permute-start.85 = (bf16[576,384]{1,0:T(8,128)(2,1)}, bf16[576,384]{1,0:T(8,128)(2,1)}, u32[]{:S(2)}, u32[]{:S(2)}) collective-permute-start(bf16[576,384]{1,0:T(8,128)(2,1)} %get-tuple-element.312), channel_id=1, source_target_pairs={{0,16},{16,0},{1,17},{17,1},{2,18},{18,2},{3,19},{19,3},{4,20},{20... | collective-permute-start | bytes 1327112 | tf_op jit(solution)/shard_map/ppermute | solution.py:645
  727.7 19.1 %collective-permute-start.86 = (bf16[8,1,192,128]{3,2,1,0:T(8,128)(2,1)}, bf16[8,1,192,128]{3,2,1,0:T(8,128)(2,1)S(1)}, u32[]{:S(2)}, u32[]{:S(2)}) collective-permute-start(bf16[8,1,192,128]{3,2,1,0:T(8,128)(2,1)} %get-tuple-element.193), channel_id=1, source_target_pairs={{0,1},{1,0},{2,3},{3,2},{4,5},{5,4},{6,7},{7,6},{8,9},{9,8},{10,11... | collective-permute-start | bytes 1179656 | tf_op jit(solution)/shard_map/ppermute | solution.py:649
  (201 other events, 2352.8 us)

commit v2 on v1

v2 whole, which is shorter than its diff:
```python
import math

import jax
import jax.numpy as jnp
from jax import lax
from jax.experimental import pallas as pl
from jax.experimental.pallas import tpu as pltpu
from jax.sharding import PartitionSpec as P

HEADS = 12
EPS = 1e-06
LOW = -1e30
MIB = 1024 * 1024
F32 = jnp.float32
BF16 = jnp.bfloat16
V = pl.BlockSpec(memory_space=pltpu.VMEM)
S = pl.BlockSpec(memory_space=pltpu.SMEM)
H = pl.BlockSpec(memory_space=pltpu.HBM)


def up_to(value, multiple):
    return -(-value // multiple) * multiple


def mm(left, right):
    return jnp.dot(left, right, preferred_element_type=F32)


def mm_back(left, right):
    return lax.dot_general(left, right, (((1,), (1,)), ((), ())), preferred_element_type=F32)


def mm_outer(left, right):
    return lax.dot_general(left, right, (((0,), (0,)), ((), ())), preferred_element_type=F32)


def norm_parts(values):
    centre = values - jnp.mean(values, axis=-1, keepdims=True)
    spread = jnp.mean(centre * centre, axis=-1, keepdims=True)
    scale = lax.rsqrt(spread + EPS)
    return centre * scale, scale


def norm_back(upstream, values, gain):
    unit, scale = norm_parts(values)
    scaled = upstream * gain
    first = jnp.mean(scaled, axis=-1, keepdims=True)
    second = jnp.mean(scaled * unit, axis=-1, keepdims=True)
    going = scale * (scaled - first - unit * second)
    return (
        going,
        jnp.sum(upstream * unit, axis=0, keepdims=True),
        jnp.sum(upstream, axis=0, keepdims=True),
    )


def gelu_parts(x):
    raised = jnp.exp(-0.5 * x * x)
    t = 1.0 / (1.0 + (0.3275911 * math.sqrt(0.5)) * jnp.abs(x))
    poly = t * (
        0.127414796
        + t * (-0.142248368 + t * (0.7107068705 + t * (-0.7265760135 + t * 0.5307027145)))
    )
    half = poly * raised
    phi = jnp.where(x >= 0, 1.0 - half, half)
    return x * phi, phi + x * (raised * (1.0 / math.sqrt(2.0 * math.pi)))


def column_cuts(width, parts):
    step = width // parts
    return [(slice(None), pl.ds(i * step, step)) for i in range(parts)]


def row_cuts(height, parts):
    step = height // parts
    return [(pl.ds(i * step, step), slice(None)) for i in range(parts)]


def fetch_start(mine, own, other, buffer, sems, cuts):
    for i, cut in enumerate(cuts):

        @pl.when(mine)
        def _():
            pltpu.make_async_copy(own.at[cut], buffer.at[cut], sems.at[i]).start()

        @pl.when(jnp.logical_not(mine))
        def _():
            pltpu.make_async_copy(other.at[cut], buffer.at[cut], sems.at[i]).start()


def fetch_wait(own, buffer, sems, cuts, i):
    pltpu.make_async_copy(own.at[cuts[i]], buffer.at[cuts[i]], sems.at[i]).wait()


def size_of(item):
    return math.prod(item.shape) * jnp.dtype(item.dtype).itemsize


def after_spec(item):
    return V if size_of(item) < 65536 else H


def kernel_call(body, ins, outs, scratch, args, flops, after=(), **more):
    ins, args = list(ins) + [after_spec(item) for item in after], tuple(args) + tuple(after)
    count = len(args)
    inner = body

    def body(*refs):
        inner(*refs[: count - len(after)], *refs[count:])

    held = [a for a, spec in zip(args, ins) if spec is V] + list(outs) + [s for s in scratch if hasattr(s, "dtype") and s.memory_space == pltpu.VMEM]
    need = sum(size_of(item) for item in held) + 8 * MIB
    moved = sum(size_of(a) for a in args) + sum(size_of(o) for o in outs)
    return pl.pallas_call(
        body,
        in_specs=ins,
        out_specs=[V] * len(outs),
        out_shape=outs,
        scratch_shapes=scratch,
        compiler_params=pltpu.CompilerParams(vmem_limit_bytes=need, **more),
        cost_estimate=pl.CostEstimate(flops=flops, bytes_accessed=moved, transcendentals=0),
    )(*args)


def shape(dims, kind):
    return jax.ShapeDtypeStruct(dims, kind)


def qkv_forward(layer, core, x, gain, shift, joined, own, other, after=()):
    rows, width = x.shape
    triple = own.shape[1]
    cuts = column_cuts(triple, 3)

    def body(core_ref, x_ref, gain_ref, shift_ref, joined_ref, own_ref, other_ref, normed_ref, proj_ref, buf, sems):
        mine = core_ref[0] == layer
        fetch_start(mine, own_ref, other_ref, buf, sems, cuts)
        unit, _ = norm_parts(x_ref[...].astype(F32))
        normed_ref[...] = (unit * gain_ref[...] + shift_ref[...]).astype(BF16)
        for i in range(3):
            fetch_wait(own_ref, buf, sems, cuts, i)
            cols = pl.ds(i * width, width)
            proj_ref[:, cols] = (mm(normed_ref[...], buf[:, cols]) + joined_ref[:, cols]).astype(BF16)

    return kernel_call(
        body,
        [S, V, V, V, V, H, H],
        [shape((rows, width), BF16), shape((rows, triple), BF16)],
        [pltpu.VMEM((width, triple), BF16), pltpu.SemaphoreType.DMA((3,))],
        (core, x, gain, shift, joined, own, other),
        5 * 10**9,
        after=after,
    )


def build_bias(base, out_ref, block_ref, grid, corner, crops, length, block_rows):
    lanes = base.shape[1]
    head_patch, patch_head, head_head = corner
    lane = lax.broadcasted_iota(jnp.int32, (block_rows, 256), 1)
    line = lax.broadcasted_iota(jnp.int32, (block_rows, 256), 0)
    first = jnp.where(lane == 0, head_head, head_patch)
    block_ref[...] = jnp.where(lane >= length, LOW, first)
    small = lane[:grid]
    for r in range(grid):
        off = (grid - 1 - r) * grid
        moved = base if off == 0 else pltpu.roll(base, lanes - off, 1)
        moved = moved[:grid, :256]
        value = jnp.where(small == 0, patch_head, jnp.where(small >= length, LOW, moved))
        block_ref[pl.ds(1 + grid * r, grid), :] = value
    if crops == 1:
        return
    out_ref[...] = jnp.full(out_ref.shape, LOW, F32)
    for s in range(crops):
        value = block_ref[pl.ds(0, length), :]
        if s:
            value = pltpu.roll(value, s * length, 1)
        out_ref[pl.ds(s * length, length), :] = value


def pair_bias(pair, corner_ref, bb_ref, bs_ref, big, block, small, sizes):
    crops, len_big, pad_big, slots, len_small, pad_small = sizes
    grid_big, grid_small = math.isqrt(len_big - 1), math.isqrt(len_small - 1)
    for h in range(2):
        head = pair * 2 + h
        build_bias(bb_ref[head], big.at[pl.ds(h * pad_big, pad_big)], big.at[pl.ds(h * pad_big, pad_big)], grid_big, [corner_ref[0, i, head] for i in range(3)], 1, len_big, pad_big)
        build_bias(bs_ref[head], small.at[pl.ds(h * pad_small, pad_small)], block, grid_small, [corner_ref[1, i, head] for i in range(3)], slots, len_small, block.shape[0])


def two_heads(value):
    lane = lax.broadcasted_iota(jnp.int32, (1, 128), 1)
    return jnp.concatenate([jnp.where(lane < 64, value, 0), jnp.where(lane >= 64, value, 0)], axis=0)


def one_line(value):
    count = value.shape[0] // 2
    lane = lax.broadcasted_iota(jnp.int32, (1, 128), 1)
    return jnp.where(lane < 64, value[:count], value[count:])


def attention_probs(scores):
    raised = jnp.exp(scores - jnp.max(scores, axis=-1, keepdims=True))
    return raised * (1.0 / jnp.sum(raised, axis=-1, keepdims=True))


def attention_parts(sizes):
    crops, _, pad_big, _, _, pad_small = sizes
    return [(c * pad_big, pad_big, True) for c in range(crops)] + [(crops * pad_big, pad_small, False)]


def bias_scratch(sizes):
    _, _, pad_big, _, len_small, pad_small = sizes
    return [
        pltpu.VMEM((2 * pad_big, 256), F32),
        pltpu.VMEM((up_to(len_small, 8), 256), F32),
        pltpu.VMEM((2 * pad_small, 256), F32),
    ]


def attention_forward(projected, base_big, base_small, corners, sizes, after=()):
    rows, triple = projected.shape
    width = triple // 3
    pairs = HEADS // 2
    parts = attention_parts(sizes)

    def body(corner_ref, proj_ref, bb_ref, bs_ref, out_ref, big, block, small):
        def step(pair, carry):
            pair_bias(pair, corner_ref, bb_ref, bs_ref, big, block, small, sizes)
            q, k, v = [pl.ds(pl.multiple_of(n * width + pair * 128, 128), 128) for n in range(3)]
            scores = []
            for start, count, is_big in parts:
                part = pl.ds(start, count)
                bias = big if is_big else small
                scores.append(mm_back(two_heads(proj_ref[part, q] * 0.125), proj_ref[part, k]) + bias[:, :count])
            probs = [attention_probs(item).astype(BF16) for item in scores]
            for (start, count, is_big), item in zip(parts, probs):
                part = pl.ds(start, count)
                out_ref[part, q] = one_line(mm(item, proj_ref[part, v])).astype(BF16)
            return carry

        lax.fori_loop(0, pairs, step, 0)

    return kernel_call(
        body,
        [S, V, V, V],
        [shape((rows, width), BF16)],
        bias_scratch(sizes),
        (corners, projected, base_big, base_small),
        10**10,
        after=after,
    )[0]


FF_STEP = 512


def up_forward(layer, core, attended, x, vec, up_bias, own, other, own_up, other_up, after=()):
    rows, width = x.shape
    hidden = own_up.shape[1]
    count = hidden // FF_STEP
    cuts = [(slice(None), slice(None))]
    up_cuts = column_cuts(hidden, count)

    def body(core_ref, att_ref, x_ref, vec_ref, bias_ref, own_ref, other_ref, own_up_ref, other_up_ref, branch_ref, middle_ref, normed_ref, hidden_ref, slope_ref, buf, buf_up, sems, sems_up):
        mine = core_ref[0] == layer
        fetch_start(mine, own_ref, other_ref, buf, sems, cuts)
        fetch_start(mine, own_up_ref, other_up_ref, buf_up, sems_up, up_cuts)
        fetch_wait(own_ref, buf, sems, cuts, 0)
        branch = mm(att_ref[...], buf[...]) + vec_ref[4:5, :]
        branch_ref[...] = branch.astype(BF16)
        middle = x_ref[...].astype(F32) + vec_ref[5:6, :] * branch
        middle_ref[...] = middle
        unit, _ = norm_parts(middle)
        normed_ref[...] = (unit * vec_ref[6:7, :] + vec_ref[7:8, :]).astype(BF16)
        for i in range(count):
            fetch_wait(own_up_ref, buf_up, sems_up, up_cuts, i)

        def pre_of(i):
            cols = pl.ds(i * FF_STEP, FF_STEP)
            return mm(normed_ref[...], buf_up[:, cols]) + bias_ref[:, cols]

        pre = pre_of(0)
        for i in range(count):
            following = pre_of(i + 1) if i + 1 < count else None
            value, slope = gelu_parts(pre)
            cols = pl.ds(i * FF_STEP, FF_STEP)
            hidden_ref[:, cols] = value.astype(BF16)
            slope_ref[:, cols] = slope.astype(BF16)
            pre = following

    return kernel_call(
        body,
        [S, V, V, V, V, H, H, H, H],
        [
            shape((rows, width), BF16),
            shape((rows, width), F32),
            shape((rows, width), BF16),
            shape((rows, hidden), BF16),
            shape((rows, hidden), BF16),
        ],
        [
            pltpu.VMEM((width, width), BF16),
            pltpu.VMEM((width, hidden), BF16),
            pltpu.SemaphoreType.DMA((1,)),
            pltpu.SemaphoreType.DMA((count,)),
        ],
        (core, attended, x, vec, up_bias, own, other, own_up, other_up),
        13 * 10**9,
        after=after,
    )


def down_forward(layer, core, hidden, middle, keep, vec, own, other, upstream=None, after=()):
    rows, width = middle.shape
    depth = hidden.shape[1]
    cuts = row_cuts(depth, 2)
    half = depth // 2
    extra = () if upstream is None else (upstream,)

    def body(core_ref, hidden_ref, middle_ref, keep_ref, vec_ref, *rest):
        own_ref, other_ref, y_ref, mlp_ref, buf, sems = rest[len(extra) :]
        fetch_start(core_ref[0] == layer, own_ref, other_ref, buf, sems, cuts)
        total = vec_ref[8:9, :]
        for i in range(2):
            fetch_wait(own_ref, buf, sems, cuts, i)
            part = pl.ds(i * half, half)
            total = total + mm(hidden_ref[:, part], buf[part, :])
        if extra:
            mlp_ref[...] = jnp.sum(rest[0][...].astype(F32) * keep_ref[...] * total, axis=0, keepdims=True)
        else:
            mlp_ref[...] = total.astype(BF16)
        y_ref[...] = ((middle_ref[...] + vec_ref[9:10, :] * total) * keep_ref[...]).astype(BF16)

    return kernel_call(
        body,
        [S, V, V, V, V] + [V] * len(extra) + [H, H],
        [shape((rows, width), BF16), shape((1, width), F32) if extra else shape((rows, width), BF16)],
        [pltpu.VMEM((depth, width), BF16), pltpu.SemaphoreType.DMA((2,))],
        (core, hidden, middle, keep, vec) + extra + (own, other),
        6 * 10**9,
        after=after,
    )


def mlp_backward(layer, core, upstream, keep, vec, slope, middle, branch, mlp, down, up, proj, after=()):
    rows, width = middle.shape
    depth = slope.shape[1]
    count = depth // FF_STEP
    half_cols, half_width = depth // 2, width // 2
    extra = () if mlp is None else (mlp,)
    down_cuts, up_cuts = row_cuts(depth, count), column_cuts(depth, count)
    cuts = [(slice(None), slice(None))]

    def body(core_ref, g_ref, keep_ref, vec_ref, slope_ref, middle_ref, branch_ref, *rest):
        if mlp is not None:
            mlp_ref, rest = rest[0], rest[1:]
        inner(core_ref, g_ref, keep_ref, vec_ref, slope_ref, middle_ref, branch_ref, *rest)
        if mlp is not None:
            vecs_ref = rest[11]
            vecs_ref[5:6, :] = jnp.sum(g_ref[...].astype(F32) * keep_ref[...] * mlp_ref[...].astype(F32), axis=0, keepdims=True)

    def inner(core_ref, g_ref, keep_ref, vec_ref, slope_ref, middle_ref, branch_ref, od, td, ou, tu, op, tp, gm_ref, gp_ref, gb_ref, ga_ref, gmid_ref, vecs_ref, ups_ref, low, bd, bu, bp, sd, su, sp):
        me = core_ref[0]
        mine = me == layer
        fetch_start(mine, od, td, bd, sd, down_cuts)
        fetch_start(mine, ou, tu, bu, su, up_cuts)
        fetch_start(mine, op, tp, bp, sp, cuts)
        gm = (vec_ref[9:10, :] * (g_ref[...].astype(F32) * keep_ref[...])).astype(BF16)
        low[...] = gm
        gm_ref[me] = gm[:, :half_width]
        gm_ref[1 - me] = gm[:, half_width:]
        vecs_ref[...] = jnp.zeros_like(vecs_ref)
        vecs_ref[4:5, :] = jnp.sum(gm.astype(F32), axis=0, keepdims=True)
        for i in range(count):
            fetch_wait(od, bd, sd, down_cuts, i)
        for i in range(count):
            cols = pl.ds(i * FF_STEP, FF_STEP)
            gp = (mm_back(low[...], bd[cols, :]) * slope_ref[:, cols].astype(F32)).astype(BF16)
            slot = me if 2 * i < count else 1 - me
            gp_ref[slot, :, pl.ds((i * FF_STEP) % half_cols, FF_STEP)] = gp
            ups_ref[:, cols] = jnp.sum(gp.astype(F32), axis=0, keepdims=True)
        for i in range(count):
            fetch_wait(ou, bu, su, up_cuts, i)
        back = mm_back(gp_ref[me], bu[:, :half_cols]) + mm_back(gp_ref[1 - me], bu[:, half_cols:])
        going, gain, shift = norm_back(back, middle_ref[...], vec_ref[6:7, :])
        gmid = g_ref[...].astype(F32) * keep_ref[...] + going
        gmid_ref[...] = gmid
        gb = (vec_ref[5:6, :] * gmid).astype(BF16)
        low[...] = gb
        gb_ref[me] = gb[:, :half_width]
        gb_ref[1 - me] = gb[:, half_width:]
        vecs_ref[0:1, :] = gain
        vecs_ref[1:2, :] = shift
        vecs_ref[2:3, :] = jnp.sum(gmid * branch_ref[...].astype(F32), axis=0, keepdims=True)
        vecs_ref[3:4, :] = jnp.sum(gb.astype(F32), axis=0, keepdims=True)
        fetch_wait(op, bp, sp, cuts, 0)
        ga_ref[...] = mm_back(low[...], bp[...]).astype(BF16)

    return kernel_call(
        body,
        [S, V, V, V, V, V, V] + [V] * len(extra) + [H] * 6,
        [
            shape((2, rows, half_width), BF16),
            shape((2, rows, half_cols), BF16),
            shape((2, rows, half_width), BF16),
            shape((rows, width), BF16),
            shape((rows, width), F32),
            shape((8, width), F32),
            shape((1, depth), F32),
        ],
        [
            pltpu.VMEM((rows, width), BF16),
            pltpu.VMEM((depth, width), BF16),
            pltpu.VMEM((width, depth), BF16),
            pltpu.VMEM((width, width), BF16),
            pltpu.SemaphoreType.DMA((count,)),
            pltpu.SemaphoreType.DMA((count,)),
            pltpu.SemaphoreType.DMA((1,)),
        ],
        (core, upstream, keep, vec, slope, middle, branch) + extra + down + up + proj,
        14 * 10**9,
        after=after,
    )


def attention_backward(core, projected, upstream, base_big, base_small, corners, sizes, after=()):
    rows, triple = projected.shape
    width = triple // 3
    pairs = HEADS // 2
    crops, len_big, pad_big, slots, len_small, pad_small = sizes
    grid_big, grid_small = math.isqrt(len_big - 1), math.isqrt(len_small - 1)
    half = 3 * pairs // 2

    parts = attention_parts(sizes)

    def body(core_ref, corner_ref, proj_ref, g_ref, bb_ref, bs_ref, gproj_ref, tb_ref, ts_ref, sums_ref, big, block, small, dbig, dsmall, dblock):
        dbig[...] = jnp.zeros_like(dbig)
        dsmall[...] = jnp.zeros_like(dsmall)
        dblock[...] = jnp.zeros_like(dblock)
        tb_ref[...] = jnp.zeros_like(tb_ref)
        ts_ref[...] = jnp.zeros_like(ts_ref)

        def step(pair, carry):
            pair_bias(pair, corner_ref, bb_ref, bs_ref, big, block, small, sizes)

            def place_for(which):
                place = which * pairs + pair + half * core_ref[0]
                return jnp.where(place >= 2 * half, place - 2 * half, place)

            q, k, v = [pl.ds(pl.multiple_of(n * width + pair * 128, 128), 128) for n in range(3)]
            places = [place_for(which) for which in range(3)]
            scores, gprs = [], []
            for start, count, is_big in parts:
                part = pl.ds(start, count)
                bias = big if is_big else small
                scores.append(mm_back(two_heads(proj_ref[part, q] * 0.125), proj_ref[part, k]) + bias[:, :count])
                gprs.append(mm_back(two_heads(g_ref[part, q]), proj_ref[part, v]))
            probs = [attention_probs(item) for item in scores]
            gss = [(p * (gpr - jnp.sum(p * gpr, axis=-1, keepdims=True))).astype(BF16) for p, gpr in zip(probs, gprs)]
            for n, ((start, count, is_big), p, gs) in enumerate(zip(parts, probs, gss)):
                part = pl.ds(start, count)
                dref = dbig if is_big else dsmall
                if n == 0 or not is_big:
                    dref[:, :count] = gs.astype(F32)
                else:
                    dref[:, :count] += gs.astype(F32)
                gproj_ref[places[0], part, :] = (one_line(mm(gs, proj_ref[part, k])) * 0.125).astype(BF16)
                gproj_ref[places[1], part, :] = mm_outer(gs, two_heads(proj_ref[part, q] * 0.125)).astype(BF16)
                gproj_ref[places[2], part, :] = mm_outer(p.astype(BF16), two_heads(g_ref[part, q])).astype(BF16)


            for h in range(2):
                hbig, hsmall = dbig.at[pl.ds(h * pad_big, pad_big)], dsmall.at[pl.ds(h * pad_small, pad_small)]

                def fold(dref, grid, length, out_ref):
                    lanes = out_ref.shape[2]
                    wide = lax.broadcasted_iota(jnp.int32, (grid, 256), 1)
                    inside = (wide > 0) & (wide < length)
                    total = jnp.zeros((grid, lanes), F32)
                    for r in range(grid):
                        value = jnp.where(inside, dref[pl.ds(1 + grid * r, grid), :], 0)
                        if lanes > 256:
                            value = jnp.concatenate([value, jnp.zeros((grid, lanes - 256), F32)], axis=1)
                        off = (grid - 1 - r) * grid
                        total = total + (value if off == 0 else pltpu.roll(value, off, 1))
                    out_ref[pair * 2 + h, :grid, :] = total
                    line = lax.broadcasted_iota(jnp.int32, (length, 256), 0)
                    spot = lax.broadcasted_iota(jnp.int32, (length, 256), 1)
                    value = jnp.where(spot < length, dref[pl.ds(0, length), :], 0)
                    out_ref[pair * 2 + h, grid : grid + 1, :256] = value[0:1, :]
                    out_ref[pair * 2 + h, grid + 1 : grid + 2, :256] = jnp.sum(jnp.where(line > 0, value, 0), axis=0, keepdims=True)

                fold(hbig, grid_big, len_big, tb_ref)
                total = hsmall[pl.ds(0, len_small), :]
                for s in range(1, slots):
                    total = total + pltpu.roll(hsmall[pl.ds(s * len_small, len_small), :], 256 - s * len_small, 1)
                dblock[pl.ds(0, len_small), :] = total
                fold(dblock, grid_small, len_small, ts_ref)
            for n, which in ((0, 0), (1, 2)):
                sums_ref[n : n + 1, q] = jnp.sum(gproj_ref[places[which]].astype(F32), axis=0, keepdims=True)
            return carry

        lax.fori_loop(0, pairs, step, 0)

    return kernel_call(
        body,
        [S, S, V, V, V, V],
        [
            shape((2 * half, rows, 128), BF16),
            shape((HEADS, 16, 512), F32),
            shape((HEADS, 8, 256), F32),
            shape((2, width), F32),
        ],
        bias_scratch(sizes)
        + [
            pltpu.VMEM((2 * pad_big, 256), F32),
            pltpu.VMEM((2 * pad_small, 256), F32),
            pltpu.VMEM((up_to(len_small, 8), 256), F32),
        ],
        (core, corners, projected, upstream, base_big, base_small),
        15 * 10**9,
        after=after,
    )


def qkv_backward(layer, core, gproj, x, gmid, gain, own, other, after=()):
    rows, width = x.shape
    blocks = gproj.shape[0]
    triple = blocks * 128
    cuts = column_cuts(triple, 3)
    group = blocks // 3

    def body(core_ref, gproj_ref, x_ref, gmid_ref, gain_ref, own_ref, other_ref, gx_ref, vecs_ref, buf, acc, sems):
        me = core_ref[0]
        fetch_start(me == layer, own_ref, other_ref, buf, sems, cuts)
        for i in range(3):
            fetch_wait(own_ref, buf, sems, cuts, i)
            places = [n + (blocks // 2) * me for n in range(i * group, (i + 1) * group)]
            places = [jnp.where(place >= blocks, place - blocks, place) for place in places]
            joined = jnp.concatenate([gproj_ref[place] for place in places], axis=1)
            more = mm_back(joined, buf[:, pl.ds(i * width, width)])
            if i == 0:
                acc[...] = more
            else:
                acc[...] += more
        going, gain_sum, shift_sum = norm_back(acc[...], x_ref[...].astype(F32), gain_ref[...])
        gx_ref[...] = (gmid_ref[...] + going).astype(BF16)
        vecs_ref[0:1, :] = gain_sum
        vecs_ref[1:2, :] = shift_sum

    return kernel_call(
        body,
        [S, V, V, V, V, H, H],
        [shape((rows, width), BF16), shape((2, width), F32)],
        [
            pltpu.VMEM((width, triple), BF16),
            pltpu.VMEM((rows, width), F32),
            pltpu.SemaphoreType.DMA((3,)),
        ],
        (core, gproj, x, gmid, gain, own, other),
        5 * 10**9,
        after=after,
    )


def place_of(relative, order):
    place = 0
    for bit in order:
        place = place * 2 + ((relative >> bit) & 1)
    return place


def weight_grad(where, orders, parts, flops, after=()):
    devices = 1 << len(orders[0])
    pieces = len(orders)
    rows = parts[0][0].shape[0]
    tiles = [part[2].shape[0] if part[2].ndim == 3 else part[2].shape[1] // 128 for part in parts]
    counts = [count // pieces for count in tiles]
    subs = sum(counts)
    block = parts[0][0].shape[1] // devices
    half = devices // 2

    def body(where_ref, *refs):
        ins, refs = refs[: 4 * len(parts)], refs[4 * len(parts) + len(after) :]
        outs, refs = refs[: 2 * pieces], refs[2 * pieces :]
        held, refs = refs[:pieces], refs[pieces:]
        sems = refs[0]
        me = where_ref[1]
        places = [[place_of(j ^ me, order) for j in range(devices)] for order in orders]

        def columns(ref, low, high):
            if len(ref.shape) == 3:
                return jnp.concatenate([ref[t] for t in range(low, high)], axis=1)
            return ref[:, low * 128 : high * 128]

        def copies(p):
            return [
                pltpu.make_async_copy(held[p].at[pl.ds(0, half)], outs[2 * p], sems.at[2 * p]),
                pltpu.make_async_copy(held[p].at[pl.ds(half, half)], outs[2 * p + 1], sems.at[2 * p + 1]),
            ]

        sub = 0
        for n, part in enumerate(parts):
            xo, xt, go, gt = ins[4 * n : 4 * n + 4]
            width = xo.shape[1]

            def put(value, line, tile, n=n, sub=sub):
                p, at = tile // counts[n], tile % counts[n]
                held[p][places[p][line], sub + at] = value

            if part[4]:
                right = jnp.concatenate([columns(go, 0, tiles[n]), columns(gt, 0, tiles[n])], axis=0)
                step = 768
                for start in range(0, width, step):
                    cut = pl.ds(start, step)
                    left = jnp.concatenate([xo[:, cut], xt[:, cut]], axis=0)
                    value = mm_outer(right, left).astype(BF16).T
                    for j in range(step // block):
                        for t in range(tiles[n]):
                            put(value[j * block : (j + 1) * block, t * 128 : (t + 1) * 128], start // block + j, t)
                for p in range(pieces):
                    if n + 1 == len(parts):
                        for copy in copies(p):
                            copy.start()
            else:
                left = jnp.concatenate([xo[...], xt[...]], axis=0).T
                done = 0
                for low in range(0, tiles[n], 4):
                    high = min(low + 4, tiles[n])
                    value = mm(left, jnp.concatenate([columns(go, low, high), columns(gt, low, high)], axis=0))
                    for j in range(devices):
                        for t in range(low, high):
                            put(value[j * block : (j + 1) * block, (t - low) * 128 : (t - low + 1) * 128].astype(BF16), j, t)
                    while n + 1 == len(parts) and done < pieces and (done + 1) * counts[n] <= high:
                        for copy in copies(done):
                            copy.start()
                        done += 1
            sub += counts[n]
        for p in range(pieces):
            for copy in copies(p):
                copy.wait()

    out = shape((half, subs, block, 128), BF16)
    args = [item for part in parts for item in part[:4]]
    return pl.pallas_call(
        body,
        in_specs=[S] + [V] * len(args) + [after_spec(item) for item in after],
        out_specs=[H] * (2 * pieces),
        out_shape=[out] * (2 * pieces),
        scratch_shapes=[pltpu.VMEM((devices, subs, block, 128), BF16)] * pieces
        + [pltpu.SemaphoreType.DMA((2 * pieces,))],
        compiler_params=pltpu.CompilerParams(vmem_limit_bytes=sum(size_of(a) for a in args) + 16 * MIB),
        cost_estimate=pl.CostEstimate(flops=flops, bytes_accessed=sum(size_of(a) for a in args), transcendentals=0),
    )(where, *args, *after)


TALL, WIDE, LAST = 11 * 10**9, 9 * 10**9, 10 * 10**9


def add_stage(items, after):
    args, outs, plan = [], [], []
    for item in items:
        kept, came, how = item
        if how == "last":
            plan.append((how, len(args), len(kept), len(outs)))
            outs.append(shape((len(kept),) + kept[0].shape[1:], F32))
            args += list(kept) + list(came)
        else:
            plan.append((how, len(args), 1, len(outs)))
            if how == "halves":
                half = shape((kept.shape[0] // 2,) + kept.shape[1:], BF16)
                outs += [half, half]
            else:
                outs.append(shape(kept.shape, F32))
            args += [kept, came]

    def body(*refs):
        ins, results = refs[: len(args)], refs[len(args) :]
        for how, at, count, to in plan:
            if how == "last":
                for n in range(count):
                    results[to][n] = ins[at + n][0].astype(F32) + ins[at + count + n][0].astype(F32)
            elif how == "whole":
                results[to][...] = ins[at][...] + ins[at + 1][...]
            else:
                half = outs[to].shape[0]
                for n in range(2):
                    cut = pl.ds(n * half, half)
                    results[to + n][...] = (ins[at][cut].astype(F32) + ins[at + 1][cut].astype(F32)).astype(BF16)
        results[-1][...] = jnp.zeros((8, 128), F32)

    made = kernel_call(body, [V] * len(args), outs + [shape((8, 128), F32)], [], tuple(args), 10**9, after=after)
    results = []
    for how, _, _, to in plan:
        results.append((made[to], made[to + 1]) if how == "halves" else made[to])
    return results, made[-1]


class Scatter:
    def __init__(self, made, orders):
        self.keeps, self.sends, self.orders = list(made[0::2]), list(made[1::2]), orders
        self.step, self.result = 0, None
        self.launch()

    def launch(self):
        self.came = [across(send, order[self.step]) for send, order in zip(self.sends, self.orders)]

    def items(self):
        if self.step + 1 == len(self.orders[0]):
            return [(self.keeps, self.came, "last")]
        return [(keep, came, "halves") for keep, came in zip(self.keeps, self.came)]

    def take(self, results):
        self.step += 1
        if self.step == len(self.orders[0]):
            self.result = results[0]
            return
        self.keeps, self.sends = [r[0] for r in results], [r[1] for r in results]
        self.launch()


class Total:
    def __init__(self, value, bits):
        self.value, self.bits, self.step, self.result = value, bits, 0, None
        self.came = swap(value)

    def items(self):
        return [(self.value, self.came, "whole")]

    def take(self, results):
        self.value = results[0]
        if self.step == self.bits:
            self.result = self.value
            return
        self.came = across(self.value, self.step)
        self.step += 1


def advance(groups, after):
    groups = [group for group in groups if group.result is None]
    if not groups:
        return after[0]
    items = [group.items() for group in groups]
    results, token = add_stage([item for part in items for item in part], after)
    for group, part in zip(groups, items):
        group.take(results[: len(part)])
        results = results[len(part) :]
    return token


def gather_vectors(parts, after):
    width = parts[0][0].shape[1]
    args = tuple(item for part in parts for item in part)
    count = len(parts[0])

    def body(*refs):
        out = refs[-1]
        out[...] = jnp.zeros_like(out)
        for layer in range(2):
            vecs1, qv, vecs2, scale, ups = refs[layer * count : layer * count + count]
            out[layer, 0:2] = vecs1[...]
            out[layer, 2:4] = qv[...]
            out[layer, 4:5] = vecs2[3:4]
            out[layer, 5:6] = vecs2[2:3]
            out[layer, 6:8] = vecs2[0:2]
            out[layer, 8:9] = vecs2[4:5]
            out[layer, 9:10] = scale[...]
            for n in range(ups.shape[1] // width):
                out[layer, 10 + n : 11 + n] = ups[:, n * width : (n + 1) * width]

    return kernel_call(body, [V] * len(args), [shape((2, 16, width), F32)], [], args, 10**9, after=after)[0]


def arrange_rows(core, own, came, sizes, after):
    crops, len_big, pad_big, slots, len_small, pad_small = sizes
    width = own[0].shape[1]
    split = crops * pad_big

    def body(core_ref, own0, own1, came0, came1, out_big, out_small):
        me = core_ref[0]

        def put(place, ref):
            for c in range(crops):
                out_big[0, place, c] = ref[pl.ds(c * pad_big, len_big), :]
            rest = ref[pl.ds(split, pad_small), :].astype(F32)
            for s in range(slots):
                out_small[0, place, s] = rest[s * len_small : (s + 1) * len_small].astype(BF16)

        @pl.when(me == 0)
        def _():
            put(0, own0)
            put(1, came0)

        @pl.when(me == 1)
        def _():
            put(1, own1)
            put(0, came1)

    return kernel_call(
        body,
        [S, V, V, V, V],
        [shape((1, 2, crops, len_big, width), BF16), shape((1, 2, slots, len_small, width), BF16)],
        [],
        (core, *own, *came),
        4 * 10**9,
        after=after,
    )


def arrange_grads(core, sums, came, block, width):
    pieces = sums[0][0].shape[0]
    tall_rows = sums[0][0].shape[2]
    subs = sums[0][1].shape[1]
    args = tuple(item for part in (*sums, *came) for item in part)

    def body(core_ref, *refs):
        down, up, proj, qkv = refs[12:]

        def put(half, tall, wide, last):
            for p in range(pieces):
                down[0, :, pl.ds((half * pieces + p) * 128, 128)] = tall[p, 0]
                proj[0, :, pl.ds((half * pieces + p) * 128, 128)] = last[p, 0]
                for t in range(subs):
                    up[0, :, pl.ds(((half * pieces + p) * subs + t) * 128, 128)] = wide[p, t]
                for t in range(subs - 1):
                    qkv[0, :, pl.ds(((half * pieces + p) * (subs - 1) + t) * 128, 128)] = last[p, 1 + t]

        @pl.when(core_ref[0] == 0)
        def _():
            put(0, *refs[0:3])
            put(1, *refs[6:9])

        @pl.when(core_ref[0] == 1)
        def _():
            put(1, *refs[3:6])
            put(0, *refs[9:12])

    return kernel_call(
        body,
        [S] + [V] * len(args),
        [
            shape((1, tall_rows, width), F32),
            shape((1, block, 2 * pieces * subs * 128), F32),
            shape((1, block, width), F32),
            shape((1, block, 2 * pieces * (subs - 1) * 128), F32),
        ],
        [],
        (core, *args),
        2 * 10**9,
    )


def swap(value):
    return lax.ppermute(value, "section", [(0, 1), (1, 0)])


def across(value, bit):
    return lax.ppermute(value, "dp", [(i, i ^ (1 << bit)) for i in range(lax.axis_size("dp"))])


def hand_over(value, layer):
    return lax.ppermute(value, "section", [(1 - layer, layer)])


HEAD_ROWS = 16


def table_lines(table, grid):
    layers, _, heads = table.shape
    side = 2 * grid - 1
    square = table[:, : side * side].reshape(layers, side, side, heads)[:, ::-1, ::-1]
    lines = jnp.transpose(square, (1, 0, 3, 2))
    lines = jnp.pad(lines, ((0, 0), (0, 0), (0, HEAD_ROWS - heads), (0, 128 - side)))
    return lines.reshape(side, layers * HEAD_ROWS, 128)


def table_bases(big, small, grids):
    heads = big.shape[1]

    def body(big_ref, small_ref, out_big, out_small):
        lane = lax.broadcasted_iota(jnp.int32, (heads, 128), 1)
        for ref, out, grid in ((big_ref, out_big, grids[0]), (small_ref, out_small, grids[1])):
            for r in range(grid):
                tiles = [jnp.zeros((heads, 128), F32) for _ in range(out.shape[2] // 128)]
                for d in range(2 * grid - 1):
                    low = 1 + d * grid
                    moved = pltpu.roll(ref[d], (low - (grid - 1 - r)) % 128, 1)
                    tile, at = low // 128, low % 128
                    tiles[tile] = jnp.where((lane >= at) & (lane < at + grid), moved, tiles[tile])
                    if at + grid > 128:
                        tiles[tile + 1] = jnp.where(lane < at + grid - 128, moved, tiles[tile + 1])
                out[r] = jnp.concatenate(tiles, axis=1)

    return kernel_call(
        body,
        [V, V],
        [shape((grids[0], heads, 512), F32), shape((grids[1], heads, 256), F32)],
        [],
        (big, small),
        3 * 10**9,
    )


def table_folds(big, small, grids, lengths, after):
    heads = big.shape[1]
    counts = [-(-(2 * grid - 1) // 4) for grid in grids]

    def body(big_ref, small_ref, out):
        lane = lax.broadcasted_iota(jnp.int32, (heads, 128), 1)
        base = 0
        ends = []
        for ref, grid, count, length in zip((big_ref, small_ref), grids, counts, lengths):
            for line in range(count):
                total = jnp.zeros((heads, 128), F32)
                for d in range(4 * line, min(4 * line + 4, 2 * grid - 1)):
                    low = 1 + d * grid
                    tile, at = low // 128, low % 128
                    for r in range(grid):
                        to = 32 * (d % 4) + grid - 1 - r
                        moved = ref[r, :, tile * 128 : tile * 128 + 128]
                        if at + grid > 128:
                            moved = jnp.where(lane >= at, moved, ref[r, :, tile * 128 + 128 : tile * 128 + 256])
                        shift = (to - at) % 128
                        moved = pltpu.roll(moved, shift, 1) if shift else moved
                        total = total + jnp.where((lane >= to) & (lane < to + grid), moved, 0)
                out[base + line] = total
            base += count
            first, second = ref[grid], ref[grid + 1]
            wide = lax.broadcasted_iota(jnp.int32, first.shape, 1)
            ends.append(jnp.sum(jnp.where((wide > 0) & (wide < length), first, 0), axis=1, keepdims=True))
            ends.append(second[:, 0:1])
            ends.append(first[:, 0:1])
        last = out[base - 1]
        for n, end in enumerate(ends):
            last = jnp.where(lane == 96 + n, end, last)
        out[base - 1] = last

    return kernel_call(body, [V, V], [shape((sum(counts), heads, 128), F32)], [], (big, small), 3 * 10**9, after=after)[0]


def table_grads(folded, grids, heads):
    grads, base = [], 0
    for n, grid in enumerate(grids):
        side = 2 * grid - 1
        count = -(-side // 4)
        lines = folded[base : base + count, :heads].reshape(count, heads, 4, 32)
        lines = jnp.transpose(lines, (0, 2, 3, 1)).reshape(count * 4, 32, heads)[:side, :side]
        ends = jnp.transpose(folded[-1, :heads, 96 + 3 * n : 99 + 3 * n])
        grads.append(jnp.concatenate([lines[::-1, ::-1].reshape(side * side, heads), ends]))
        base += count
    return grads


def body(input_big, input_small, small_counts, cotangent_big, cotangent_small, norm1_gain, norm1_bias, qkv_weight, query_bias, value_bias, table_big, table_small, proj_weight, proj_bias, attn_scale, norm2_gain, norm2_bias, up_weight, up_bias, down_weight, down_bias, mlp_scale):
    micro, crops, len_big, width = input_big.shape
    slots_all, len_small = input_small.shape[1], input_small.shape[2]
    slots = slots_all // small_counts.shape[1]
    grid_big, grid_small = math.isqrt(len_big - 1), math.isqrt(len_small - 1)
    pad_big = up_to(len_big, 16)
    real_small = slots_all * len_small
    pad_small = up_to(real_small, 16)
    split = crops * pad_big
    rows = split + pad_small
    sizes = (crops, len_big, pad_big, slots_all, len_small, pad_small)
    devices = lax.axis_size("dp")
    bits = devices.bit_length() - 1
    core = lax.axis_index("section")
    place = lax.axis_index("dp")
    where = jnp.stack([core, place]).astype(jnp.int32)
    first = core == 0

    def join(big, small):
        big = lax.dynamic_index_in_dim(big, core, 0, keepdims=False)
        small = lax.dynamic_index_in_dim(small, core, 0, keepdims=False)
        big = jnp.pad(big, ((0, 0), (0, pad_big - len_big), (0, 0))).reshape(split, width)
        small = jnp.pad(small.reshape(real_small, width), ((0, pad_small - real_small), (0, 0)))
        return jnp.concatenate([big, small])

    x0 = join(input_big, input_small)
    cotangent = join(cotangent_big, cotangent_small)
    counts = lax.dynamic_index_in_dim(small_counts, core, 0, keepdims=False)
    line = jnp.arange(rows, dtype=jnp.int32)
    spot = line - split
    limit = jnp.repeat(counts, slots * len_small, total_repeat_length=real_small)
    small_keep = (jnp.arange(real_small, dtype=jnp.int32) // len_small % slots < limit).astype(F32)
    keep = jnp.where(line < split, (line % pad_big < len_big).astype(F32), jnp.pad(small_keep, (split, pad_small - real_small)))
    keep = keep[:, None]

    vec_own = jnp.concatenate(
        [norm1_gain, norm1_bias, query_bias, value_bias, proj_bias, attn_scale, norm2_gain, norm2_bias, down_bias, mlp_scale, up_bias.reshape(-1, width)]
    )
    tables_own = jnp.concatenate([table_big[0], table_small[0]])
    vec_other, tables_other = swap(vec_own), swap(tables_own)
    qkv = (qkv_weight[0], swap(qkv_weight[0]))
    proj = (proj_weight[0], swap(proj_weight[0]))
    up = (up_weight[0], swap(up_weight[0]))
    down = (down_weight[0], swap(down_weight[0]))

    grids, lengths = (grid_big, grid_small), (len_big, len_small)
    entries_big = table_big.shape[1]
    both = jnp.stack([jnp.where(first, tables_own, tables_other), jnp.where(first, tables_other, tables_own)])
    both_big, both_small = both[:, :entries_big], both[:, entries_big:]
    base_big, base_small = table_bases(table_lines(both_big, grid_big), table_lines(both_small, grid_small), grids)

    def by_head(base, rows):
        base = base.reshape(base.shape[0], 2, HEAD_ROWS, -1)[:, :, :HEADS]
        return jnp.pad(jnp.transpose(base, (1, 2, 0, 3)), ((0, 0), (0, 0), (0, rows - base.shape[0]), (0, 0)))

    base_big, base_small = by_head(base_big, 16), by_head(base_small, 8)
    layers = []
    for layer in range(2):
        vec = jnp.where(core == layer, vec_own, vec_other)
        ups = vec[10:].reshape(1, -1)
        joined = jnp.concatenate([vec[2:3], jnp.zeros_like(vec[2:3]), vec[3:4]], axis=1)
        corners = jnp.stack([both_big[layer, -3:], both_small[layer, -3:]])
        layers.append((vec, ups, joined, corners, base_big[layer], base_small[layer]))

    saved = []
    x = x0
    for layer in range(2):
        vec, ups, joined, corners, big, small = layers[layer]
        normed, projected = qkv_forward(layer, where, x, vec[0:1], vec[1:2], joined, *qkv)
        attended = attention_forward(projected, big, small, corners, sizes)
        branch, middle, normed2, hidden, slope = up_forward(layer, where, attended, x, vec, ups, *proj, *up)
        saved.append((x, normed, projected, attended, branch, middle, normed2, hidden, slope))
        if layer == 0:
            x, mlp0 = down_forward(layer, where, hidden, middle, keep, vec, *down)

    orders = [list(range(bits)), [1, 0] + list(range(2, bits)), [2, 0, 1] + list(range(3, bits))]

    def mlp_part(layer, g, mlp, after=()):
        vec = layers[layer][0]
        x, normed, projected, attended, branch, middle, normed2, hidden, slope = saved[layer]
        return mlp_backward(layer, where, g, keep, vec, slope, middle, branch, mlp, down, up, proj, after=after)

    def attention_part(layer, ga, after):
        _, _, _, corners, big, small = layers[layer]
        return attention_backward(where, saved[layer][2], ga, big, small, corners, sizes, after=after)

    def qkv_part(layer, gproj, gmid, after):
        return qkv_backward(layer, where, gproj, saved[layer][0], gmid, layers[layer][0][0:1], *qkv, after=after)

    def tall_grad(layer, others, gm, gm_other, after):
        part = (saved[layer][7], others[0], gm[0], gm_other, True)
        return weight_grad(where, orders, [part], TALL, after)

    def wide_grad(layer, others, gp, gp_other, after):
        part = (saved[layer][6], others[1], gp[0], gp_other, False)
        return weight_grad(where, orders, [part], WIDE, after)

    def last_grad(layer, others, gb, gb_other, gproj, gproj_other, after):
        parts = [
            (saved[layer][3], others[2], gb[0], gb_other, False),
            (saved[layer][1], others[3], gproj[: gproj.shape[0] // 2], gproj_other, False),
        ]
        return weight_grad(where, orders, parts, LAST, after)

    others = [[swap(saved[layer][n]) for n in (7, 6, 3, 1)] for layer in range(2)]
    came_y0 = hand_over(saved[1][0], 0)

    gm, gp, gb, ga, gmid, vecs2_1, ups_1 = mlp_part(1, cotangent, None)
    gm_other, gp_other, gb_other = swap(gm[1]), swap(gp[1]), swap(gb[1])
    made = tall_grad(1, others[1], gm, gm_other, (ups_1,))
    tall1 = Scatter(made, orders)
    made = wide_grad(1, others[1], gp, gp_other, made[:1])
    wide1 = Scatter(made, orders)
    gproj, fold_big1, fold_small1, qv_1 = attention_part(1, ga, made[:1])
    gproj_other = swap(gproj[gproj.shape[0] // 2 :])
    token = advance([tall1, wide1], (qv_1,))
    gx1, vecs1_1 = qkv_part(1, gproj, gmid, (token,))
    came_gx1 = hand_over(gx1, 1)
    made = last_grad(1, others[1], gb, gb_other, gproj, gproj_other, (vecs1_1,))
    last1 = Scatter(made, orders)
    token = advance([tall1, wide1], made[:1])

    gm, gp, gb, ga, gmid, vecs2_0, ups_0 = mlp_part(0, gx1, mlp0, (token,))
    gm_other, gp_other, gb_other = swap(gm[1]), swap(gp[1]), swap(gb[1])
    token = advance([tall1, wide1, last1], (ups_0,))
    made = tall_grad(0, others[0], gm, gm_other, (token,))
    tall0 = Scatter(made, orders)
    token = advance([tall1, wide1, last1], made[:1])
    made = wide_grad(0, others[0], gp, gp_other, (token,))
    wide0 = Scatter(made, orders)
    token = advance([last1], made[:1])
    gproj, fold_big0, fold_small0, qv_0 = attention_part(0, ga, (token,))
    gproj_other = swap(gproj[gproj.shape[0] // 2 :])
    token = advance([last1, tall0, wide0], (qv_0,))
    y1, scale_1 = down_forward(1, where, saved[1][7], saved[1][5], keep, layers[1][0], *down, upstream=cotangent, after=(token,))
    came_y1 = hand_over(y1, 1)
    made = last_grad(0, others[0], gb, gb_other, gproj, gproj_other, (scale_1,))
    last0 = Scatter(made, orders)
    token = advance([tall0, wide0], made[:1])
    gx0, vecs1_0 = qkv_part(0, gproj, gmid, (token,))
    came_gx0 = hand_over(gx0, 0)

    def by_line(zero, one):
        both = jnp.pad(jnp.stack([zero, one]), ((0, 0), (0, HEAD_ROWS - HEADS), (0, 0), (0, 0)))
        return jnp.transpose(both, (2, 0, 1, 3)).reshape(zero.shape[1], 2 * HEAD_ROWS, -1)

    folded = table_folds(by_line(fold_big0, fold_big1), by_line(fold_small0, fold_small1), grids, lengths, (vecs1_0,))
    tables = Total(folded, bits)
    vectors = gather_vectors(
        [(vecs1_0, qv_0, vecs2_0, vecs2_0[5:6], ups_0), (vecs1_1, qv_1, vecs2_1, scale_1, ups_1)], ()
    )
    vectors = Total(vectors, bits)
    layer_big, layer_small = arrange_rows(where, (saved[1][0], y1), (came_y0, came_y1), sizes, (folded,))
    groups = [last0, tall0, wide0, tables, vectors, last1, tall1, wide1]
    token = advance(groups, (layer_small[0, 0, 0, :8, :128],))
    token = advance(groups, (token,))
    grad_big, grad_small = arrange_rows(where, (gx0, gx1), (came_gx0, came_gx1), sizes, (token,))
    token = grad_small[0, 0, 0, :8, :128]
    while any(group.result is None for group in groups):
        token = advance(groups, (token,))

    sums = [[group.result for group in part] for part in ((tall0, wide0, last0), (tall1, wide1, last1))]
    came = [[hand_over(item, layer) for item in sums[layer]] for layer in range(2)]
    block = width // devices
    grad_down, grad_up, grad_proj, grad_qkv = arrange_grads(where, sums, came, block, width)

    ff = up_bias.shape[1] // width
    mine = lax.dynamic_index_in_dim(vectors.result, core, 0, keepdims=False)
    lines = lax.dynamic_slice(mine, (0, place * block), (10, block))
    grad_up_bias = lax.dynamic_slice(mine[10 : 10 + ff].reshape(1, -1), (0, place * ff * block), (1, ff * block))

    def vector(row):
        return lines[row : row + 1]

    folded = tables.result.reshape(-1, 2, HEAD_ROWS, 128)
    folded = lax.dynamic_index_in_dim(folded, core, 1, keepdims=False)
    grad_table_big, grad_table_small = [item[None] for item in table_grads(folded, grids, HEADS)]
    return (
        layer_big,
        layer_small,
        grad_big,
        grad_small,
        vector(0),
        vector(1),
        grad_qkv,
        vector(2),
        vector(3),
        grad_table_big,
        grad_table_small,
        grad_proj,
        vector(4),
        vector(5),
        vector(6),
        vector(7),
        grad_up,
        grad_up_bias,
        grad_down,
        vector(8),
        vector(9),
    )


def solution(mesh):
    row = P("section", None)
    whole = P("section", None, None)
    dp4 = P(None, "dp", None, None)
    in_specs = (dp4, dp4, P(None, "dp"), dp4, dp4, row, row, whole, row, row, whole, whole, whole, row, row, row, row, whole, row, whole, row, row)
    out5 = P("section", None, "dp", None, None)
    vec = P("section", "dp")
    mat = P("section", "dp", None)
    out_specs = (out5, out5, out5, out5, vec, vec, mat, vec, vec, whole, whole, mat, vec, vec, vec, vec, mat, vec, mat, vec, vec)
    return jax.shard_map(body, mesh=mesh, in_specs=in_specs, out_specs=out_specs, check_vma=False)
```

time: 793 us -> 452 us (0.57)
  local copies, waits for them, and re-layouts: 178 us -> 48.3 us
  Pallas kernels: 310 us -> 182 us
  waiting for transfers between devices: 158 us -> 83.8 us
  other arithmetic: 33.7 us -> 5.22 us
  starting transfers between devices: 100 us -> 121 us
    ppermute x80, waiting for transfers between devices: 150 us -> 79.7 us  [across(): lax.ppermute(value, 'dp', [(i, i ^ 1 << bit) for i in range(lax.axis_size...]
    slice x145 -> x9, local copies, waits for them, and re-layouts: 67.6 us -> 1.78 us  [the longest x1 0.71 us: body(): corners = jnp.stack([both_big[layer, -3:], both_small[layer, -3:]])]
    pallas_call x14 -> x32, Pallas kernels: 208 us -> 142 us  [kernel_call(): pl.pallas_call(body, in_specs=ins, out_specs=[V] * len(outs), out_shape=o...]
    pallas_call x6, Pallas kernels: 102 us -> 39.5 us  [weight_grad(): pl.pallas_call(body, in_specs=[S] + [V] * len(args) + [after_spec(item) f...]
    reshape x34 -> x4, local copies, waits for them, and re-layouts: 20.1 us -> 0.68 us  [the longest x2 0.45 us: table_lines(): table[:, :side * side].reshape(layers, side, side, heads)[:, ::-1, ::-1]]
    ppermute x0 -> x10, starting transfers between devices: none -> 17.4 us  [hand_over(): return lax.ppermute(value, 'section', [(1 - layer, layer)])]
    unnamed x319 -> x230, local copies, waits for them, and re-layouts: 44.5 us -> 31.8 us
    another operation x25 -> x3, local copies, waits for them, and re-layouts: 12.1 us -> 0.36 us  [the longest x2 0.36 us: body(): jnp.stack([jnp.where(first, tables_own, tables_other), jnp.where(first, t...]
  transfers between devices with their start and end apart: 115 -> 114, of which waited for: 69 -> 40; matrix products, arithmetic and copies ran while one was open for 26% -> 6% of each run, Pallas kernels for 36% -> 32%
where the time goes in v2:
time: 452 us; the launch traced here: 444 us
  Pallas kernels  182 us (40%)
  starting transfers between devices  121 us (27%)
  waiting for transfers between devices  83.8 us (19%)
  local copies, waits for them, and re-layouts  48.3 us (11%)
  other arithmetic  5.22 us (1%)
    pallas_call x32, Pallas kernels, kernel_call(): pl.pallas_call(body, in_specs=ins, out_specs=[V] * len(outs), out_shape=o...  142 us
    ppermute x80, starting transfers between devices, across(): lax.ppermute(value, 'dp', [(i, i ^ 1 << bit) for i in range(lax.axis_size...  94.6 us
    ppermute x80, waiting for transfers between devices, across(): lax.ppermute(value, 'dp', [(i, i ^ 1 << bit) for i in range(lax.axis_size...  79.7 us
    pallas_call x6, Pallas kernels, weight_grad(): pl.pallas_call(body, in_specs=[S] + [V] * len(args) + [after_spec(item) f...  39.5 us
    unnamed x230, local copies, waits for them, and re-layouts  31.8 us
    ppermute x10, starting transfers between devices, hand_over(): return lax.ppermute(value, 'section', [(1 - layer, layer)])  17.4 us
    ppermute x24, starting transfers between devices, swap(): return lax.ppermute(value, 'section', [(0, 1), (1, 0)])  9.5 us
  transfers between devices with their start and end apart: 114, of which 40 were waited for; matrix products, arithmetic and copies ran while one was open for 6% of the time, Pallas kernels for 32%

profile of v2, /device:TPU:0, one launch (start us, length us, event | category | flops | bytes accessed | tf_op | source)
XLA Modules:
  0.0 443.7 jit_solution(18339500798790924655)
XLA Ops:
  22.1 4.5 %shard_map.373 = (bf16[576,768]{1,0:T(8,128)(2,1)S(1)}, bf16[576,2304]{1,0:T(8,128)(2,1)S(1)}) custom-call(s32[2]{0:T(128)S(1)} %pad_add_fusion.refs_0_.where_ref, bf16[576,768]{1,0:T(8,128)(2,1)S(1)} %fusion.3.refs_1_.refs_2_, f32[1,768]{1,0:T(1,128)S(1)} %get-tuple-element.614.refs_2_.refs_4_, f32[1,768]{1,0:T(1,128)S(1)} %get-tuple-element.615.refs_3_, ...), custom_call_target="tpu_custom_call" | custom-call | flops 5000000000 | bytes 11516936 | tf_op jit(solution)/shard_map/pallas_call | solution.py:114
  26.7 8.8 %shard_map.375.refs_1_.refs_0_ = bf16[576,768]{1,0:T(8,128)(2,1)S(1)} custom-call(f32[2,3,12]{2,1,0:T(4,128)S(1)} %pad_maximum_fusion.5.refs_0_.refs_1_, bf16[576,2304]{1,0:T(8,128)(2,1)S(1)} %get-tuple-element.270.refs_1_.refs_2_, f32[12,16,512]{2,1,0:T(8,128)S(1)} %get-tuple-element.577.refs_2_.refs_4_, f32[12,8,256]{2,1,0:T(8,128)S(1)} %get-tuple-element.585.refs_3_.refs_5_), custom_call_target="tpu_custom_call" | custom-call | flops 10000000000 | bytes 4030752 | tf_op jit(solution)/shard_map/pallas_call | solution.py:114
  35.6 11.3 %shard_map.376 = (bf16[576,768]{1,0:T(8,128)(2,1)S(1)}, f32[576,768]{1,0:T(8,128)S(1)}, bf16[576,768]{1,0:T(8,128)(2,1)S(1)}, bf16[576,3072]{1,0:T(8,128)(2,1)S(1)}, bf16[576,3072]{1,0:T(8,128)(2,1)S(1)}) custom-call(s32[2]{0:T(128)S(1)} %pad_add_fusion.refs_0_.where_ref, bf16[576,768]{1,0:T(8,128)(2,1)S(1)} %shard_map.375.refs_1_.refs_0_, ...), custom_call_target="tpu_custom_call" | custom-call | flops 12999999488 | bytes 24238088 | tf_op jit(solution)/shard_map/pallas_call | solution.py:114
  47.9 4.9 %shard_map.377 = (bf16[576,768]{1,0:T(8,128)(2,1)S(1)}, bf16[576,768]{1,0:T(8,128)(2,1)S(1)}) custom-call(s32[2]{0:T(128)S(1)} %pad_add_fusion.refs_0_.where_ref, bf16[576,3072]{1,0:T(8,128)(2,1)S(1)} %get-tuple-element.273.refs_1_.refs_0_, f32[576,768]{1,0:T(8,128)S(1)} %get-tuple-element.274.refs_2_.refs_5_, ...), custom_call_target="tpu_custom_call" | custom-call | flops 6000000000 | bytes 16560392 | tf_op jit(solution)/shard_map/pallas_call | solution.py:114
  52.9 4.9 %shard_map.378 = (bf16[576,768]{1,0:T(8,128)(2,1)S(1)}, bf16[576,2304]{1,0:T(8,128)(2,1)S(1)}) custom-call(s32[2]{0:T(128)S(1)} %pad_add_fusion.refs_0_.where_ref, bf16[576,768]{1,0:T(8,128)(2,1)S(1)} %get-tuple-element.275.refs_1_.refs_2_, f32[1,768]{1,0:T(1,128)S(1)} %get-tuple-element.601.refs_2_.refs_4_, f32[1,768]{1,0:T(1,128)S(1)} %get-tuple-element.600.refs_3_, ...), custom_call_target="tpu_custom_call" | custom-call | flops 5000000000 | bytes 11516936 | tf_op jit(solution)/shard_map/pallas_call | solution.py:114
  57.8 8.8 %shard_map.379.refs_1_.refs_0_ = bf16[576,768]{1,0:T(8,128)(2,1)S(1)} custom-call(f32[2,3,12]{2,1,0:T(4,128)S(1)} %pad_maximum_fusion.6.refs_0_.refs_1_, bf16[576,2304]{1,0:T(8,128)(2,1)S(1)} %get-tuple-element.276.refs_1_.refs_2_, f32[12,16,512]{2,1,0:T(8,128)S(1)} %get-tuple-element.576.refs_2_.refs_4_, f32[12,8,256]{2,1,0:T(8,128)S(1)} %get-tuple-element.584.refs_3_.refs_5_), custom_call_target="tpu_custom_call" | custom-call | flops 10000000000 | bytes 4030752 | tf_op jit(solution)/shard_map/pallas_call | solution.py:114
  66.6 13.3 %shard_map.380 = (bf16[576,768]{1,0:T(8,128)(2,1)S(1)}, f32[576,768]{1,0:T(8,128)S(1)}, bf16[576,768]{1,0:T(8,128)(2,1)S(1)}, bf16[576,3072]{1,0:T(8,128)(2,1)}, bf16[576,3072]{1,0:T(8,128)(2,1)S(1)}) custom-call(s32[2]{0:T(128)S(1)} %pad_add_fusion.refs_0_.where_ref, bf16[576,768]{1,0:T(8,128)(2,1)S(1)} %shard_map.379.refs_1_.refs_0_, ...), custom_call_target="tpu_custom_call" | custom-call | flops 12999999488 | bytes 24238088 | tf_op jit(solution)/shard_map/pallas_call | solution.py:114
  84.8 5.7 %collective-permute-start.6 = (bf16[576,3072]{1,0:T(8,128)(2,1)}, bf16[576,3072]{1,0:T(8,128)(2,1)}, u32[]{:S(2)}, u32[]{:S(2)}) collective-permute-start(bf16[576,3072]{1,0:T(8,128)(2,1)} %get-tuple-element.277.refs_0_.refs_1_), channel_id=1, source_target_pairs={{0,16},{16,0},{1,17},{17,1},{2,18},{18,2},{3,19},{19,3},{4,20},{20... | collective-permute-start | bytes 10616840 | tf_op jit(solution)/shard_map/ppermute | solution.py:852
  97.4 14.0 %shard_map.381 = (bf16[2,576,384]{2,1,0:T(8,128)(2,1)S(1)}, bf16[2,576,1536]{2,1,0:T(8,128)(2,1)S(1)}, bf16[2,576,384]{2,1,0:T(8,128)(2,1)S(1)}, bf16[576,768]{1...) custom-call(s32[2]{0:T(128)S(1)} %pad_add_fusion.refs_0_.where_ref, ...), custom_call_target="tpu_custom_call" | custom-call | flops 14000000000 | bytes 36356360 | tf_op jit(solution)/shard_map/pallas_call | solution.py:114
  116.9 8.1 %shard_map.382 = (bf16[8,1,192,128]{3,2,1,0:T(8,128)(2,1)S(1)}, bf16[8,1,192,128]{3,2,1,0:T(8,128)(2,1)S(1)}, bf16[8,1,192,128]{3,2,1,0:T(8,128)(2,1)S(1)}, bf16...) custom-call(s32[2]{0:T(128)S(1)} %pad_add_fusion.refs_0_.where_ref, ...), custom_call_target="tpu_custom_call" | custom-call | flops 11000000512 | bytes 7962624 | tf_op jit(solution)/shard_map/pallas_call | solution.py:643
  125.0 5.5 %shard_map.383 = (bf16[8,4,48,128]{3,2,1,0:T(8,128)(2,1)S(1)}, bf16[8,4,48,128]{3,2,1,0:T(8,128)(2,1)S(1)}, bf16[8,4,48,128]{3,2,1,0:T(8,128)(2,1)S(1)}, bf16[8,...) custom-call(s32[2]{0:T(128)S(1)} %pad_add_fusion.refs_0_.where_ref, ...), custom_call_target="tpu_custom_call" | custom-call | flops 8999999488 | bytes 5308416 | tf_op jit(solution)/shard_map/pallas_call | solution.py:643
  134.7 12.1 %shard_map.384 = (bf16[18,576,128]{2,1,0:T(8,128)(2,1)S(1)}, f32[12,16,512]{2,1,0:T(8,128)S(1)}, f32[12,8,256]{2,1,0:T(8,128)S(1)}, f32[2,768]{1,0:T(2,128)S(1)}) custom-call(s32[2]{0:T(128)S(1)} %pad_add_fusion.refs_0_.where_ref, f32[2,3,12]{2,1,0:T(4,128)S(1)} %pad_maximum_fusion.6.refs_0_.refs_1_, bf16[576,2304]{1,0:T(8,128)(2,1)S(1)} %copy-done.75, ...), custom_call_target="tpu_custom_call" | custom-call | flops 15000000512 | bytes 7575848 | tf_op jit(solution)/shard_map/pallas_call | solution.py:114
  150.0 9.1 %collective-permute-done.15.refs_11_ = bf16[8,4,48,128]{3,2,1,0:T(8,128)(2,1)S(1)} collective-permute-done((bf16[8,4,48,128]{3,2,1,0:T(8,128)(2,1)S(1)}, bf16[8,4,48,128]{3,2,1,0:T(8,128)(2,1)S(1)}, u32[]{:S(2)}, u32[]{:S(2)}) %collective-permute-start.15) | collective-permute-done | bytes 393248 | tf_op jit(solution)/shard_map/ppermute | solution.py:856
  159.1 8.0 %collective-permute-done.10.refs_5_ = bf16[8,1,192,128]{3,2,1,0:T(8,128)(2,1)S(1)} collective-permute-done((bf16[8,1,192,128]{3,2,1,0:T(8,128)(2,1)S(1)}, bf16[8,1,192,128]{3,2,1,0:T(8,128)(2,1)S(1)}, u32[]{:S(2)}, u32[]{:S(2)}) %collective-permute-start.10) | collective-permute-done | bytes 393248 | tf_op jit(solution)/shard_map/ppermute | solution.py:856
  169.8 6.4 %shard_map.386 = (bf16[576,768]{1,0:T(8,128)(2,1)S(1)}, f32[2,768]{1,0:T(2,128)S(1)}) custom-call(s32[2]{0:T(128)S(1)} %pad_add_fusion.refs_0_.where_ref, bf16[18,576,128]{2,1,0:T(8,128)(2,1)S(1)} %get-tuple-element.313.refs_1_, bf16[576,768]{1,0:T(8,128)(2,1)S(1)} %copy-done.17, f32[576,768]{1,0:T(8,128)S(1)} %copy-done.66, ...), custom_call_target="tpu_custom_call" | custom-call | flops 5000000000 | bytes 13284360 | tf_op jit(solution)/shard_map/pallas_call | solution.py:114
  180.9 6.6 %shard_map.387 = (bf16[8,4,48,128]{3,2,1,0:T(8,128)(2,1)S(1)}, bf16[8,4,48,128]{3,2,1,0:T(8,128)(2,1)S(1)}, bf16[8,4,48,128]{3,2,1,0:T(8,128)(2,1)S(1)}, bf16[8,...) custom-call(s32[2]{0:T(128)S(1)} %pad_add_fusion.refs_0_.where_ref, ...), custom_call_target="tpu_custom_call" | custom-call | flops 10000000000 | bytes 7077888 | tf_op jit(solution)/shard_map/pallas_call | solution.py:643
  200.9 14.1 %shard_map.389 = (bf16[2,576,384]{2,1,0:T(8,128)(2,1)S(1)}, bf16[2,576,1536]{2,1,0:T(8,128)(2,1)S(1)}, bf16[2,576,384]{2,1,0:T(8,128)(2,1)S(1)}, bf16[576,768]{1...) custom-call(s32[2]{0:T(128)S(1)} %pad_add_fusion.refs_0_.where_ref, ...), custom_call_target="tpu_custom_call" | custom-call | flops 14000000000 | bytes 37245192 | tf_op jit(solution)/shard_map/pallas_call | solution.py:114
  247.4 7.2 %shard_map.391 = (bf16[8,1,192,128]{3,2,1,0:T(8,128)(2,1)S(1)}, bf16[8,1,192,128]{3,2,1,0:T(8,128)(2,1)S(1)}, bf16[8,1,192,128]{3,2,1,0:T(8,128)(2,1)S(1)}, bf16...) custom-call(s32[2]{0:T(128)S(1)} %pad_add_fusion.refs_0_.where_ref, ...), custom_call_target="tpu_custom_call" | custom-call | flops 11000000512 | bytes 7962624 | tf_op jit(solution)/shard_map/pallas_call | solution.py:643
  259.8 5.5 %shard_map.393 = (bf16[8,4,48,128]{3,2,1,0:T(8,128)(2,1)S(1)}, bf16[8,4,48,128]{3,2,1,0:T(8,128)(2,1)S(1)}, bf16[8,4,48,128]{3,2,1,0:T(8,128)(2,1)S(1)}, bf16[8,...) custom-call(s32[2]{0:T(128)S(1)} %pad_add_fusion.refs_0_.where_ref, ...), custom_call_target="tpu_custom_call" | custom-call | flops 8999999488 | bytes 5308416 | tf_op jit(solution)/shard_map/pallas_call | solution.py:643
  269.3 12.1 %shard_map.395 = (bf16[18,576,128]{2,1,0:T(8,128)(2,1)S(1)}, f32[12,16,512]{2,1,0:T(8,128)S(1)}, f32[12,8,256]{2,1,0:T(8,128)S(1)}, f32[2,768]{1,0:T(2,128)S(1)}) custom-call(s32[2]{0:T(128)S(1)} %pad_add_fusion.refs_0_.where_ref, f32[2,3,12]{2,1,0:T(4,128)S(1)} %copy-done.7, bf16[576,2304]{1,0:T(8,128)(2,1)S(1)} %copy-done.73, ...), custom_call_target="tpu_custom_call" | custom-call | flops 15000000512 | bytes 7186728 | tf_op jit(solution)/shard_map/pallas_call | solution.py:114
  292.4 6.2 %collective-permute-done.53.refs_5_ = bf16[1,4,48,128]{3,2,1,0:T(8,128)(2,1)S(1)} collective-permute-done((bf16[1,4,48,128]{3,2,1,0:T(8,128)(2,1)S(1)}, bf16[1,4,48,128]{3,2,1,0:T(8,128)(2,1)S(1)}, u32[]{:S(2)}, u32[]{:S(2)}) %collective-permute-start.53) | collective-permute-done | bytes 49184 | tf_op jit(solution)/shard_map/ppermute | solution.py:856
  302.7 7.8 %shard_map.397 = (bf16[576,768]{1,0:T(8,128)(2,1)S(1)}, f32[1,768]{1,0:T(1,128)S(1)}) custom-call(s32[2]{0:T(128)S(1)} %pad_add_fusion.refs_0_.where_ref, bf16[576,3072]{1,0:T(8,128)(2,1)} %get-tuple-element.277.refs_0_.refs_1_, f32[576,768]{1,0:T(8,128)S(1)} %copy-done.69, f32[576,1]{1,0:T(8,128)S(1)} %broadcast_in_dim.18.refs_3_.refs_2_, ...), custom_call_target="tpu_custom_call" | custom-call | flops 6000000000 | bytes 16567560 | tf_op jit(solution)/shard_map/pallas_call | solution.py:114
  315.5 6.6 %shard_map.398 = (bf16[8,4,48,128]{3,2,1,0:T(8,128)(2,1)S(1)}, bf16[8,4,48,128]{3,2,1,0:T(8,128)(2,1)S(1)}, bf16[8,4,48,128]{3,2,1,0:T(8,128)(2,1)S(1)}, bf16[8,...) custom-call(s32[2]{0:T(128)S(1)} %pad_add_fusion.refs_0_.where_ref, ...), custom_call_target="tpu_custom_call" | custom-call | flops 10000000000 | bytes 7077888 | tf_op jit(solution)/shard_map/pallas_call | solution.py:643
  329.8 5.3 %shard_map.400 = (bf16[576,768]{1,0:T(8,128)(2,1)S(1)}, f32[2,768]{1,0:T(2,128)S(1)}) custom-call(s32[2]{0:T(128)S(1)} %pad_add_fusion.refs_0_.where_ref, bf16[18,576,128]{2,1,0:T(8,128)(2,1)S(1)} %get-tuple-element.397.refs_1_, bf16[576,768]{1,0:T(8,128)(2,1)S(1)} %fusion.3.refs_1_.refs_2_, f32[576,768]{1,0:T(8,128)S(1)} %copy-done.64, ...), custom_call_target="tpu_custom_call" | custom-call | flops 5000000000 | bytes 13284360 | tf_op jit(solution)/shard_map/pallas_call | solution.py:114
  (553 shorter events, 244.0 us)
Async XLA Ops:
  8.1 27.4 %collective-permute-start.4 = (bf16[768,3072]{1,0:T(8,128)(2,1)}, bf16[768,3072]{1,0:T(8,128)(2,1)}, u32[]{:S(2)}, u32[]{:S(2)}) collective-permute-start(bf16[768,3072]{1,0:T(8,128)(2,1)} %bitcast.154), channel_id=1, source_target_pairs={{0,16},{16,0},{1,17},{17,1},{2,18},{18,2},{3,19},{19,3},{4,20},{20... | collective-permute-start | bytes 14155784 | tf_op jit(solution)/shard_map/ppermute | solution.py:852
  8.2 27.3 %collective-permute-start.3 = (bf16[768,768]{1,0:T(8,128)(2,1)}, bf16[768,768]{1,0:T(8,128)(2,1)}, u32[]{:S(2)}, u32[]{:S(2)}) collective-permute-start(bf16[768,768]{1,0:T(8,128)(2,1)} %bitcast.175), channel_id=1, source_target_pairs={{0,16},{16,0},{1,17},{17,1},{2,18},{18,2},{3,19},{19,3},{4,20},{20... | collective-permute-start | bytes 3538952 | tf_op jit(solution)/shard_map/ppermute | solution.py:852
  14.3 33.6 %collective-permute-start.5 = (bf16[3072,768]{1,0:T(8,128)(2,1)}, bf16[3072,768]{1,0:T(8,128)(2,1)}, u32[]{:S(2)}, u32[]{:S(2)}) collective-permute-start(bf16[3072,768]{1,0:T(8,128)(2,1)} %bitcast.161), channel_id=1, source_target_pairs={{0,16},{16,0},{1,17},{17,1},{2,18},{18,2},{3,19},{19,3},{4,20},{20... | collective-permute-start | bytes 14155784 | tf_op jit(solution)/shard_map/ppermute | solution.py:852
  84.8 32.1 %collective-permute-start.6 = (bf16[576,3072]{1,0:T(8,128)(2,1)}, bf16[576,3072]{1,0:T(8,128)(2,1)}, u32[]{:S(2)}, u32[]{:S(2)}) collective-permute-start(bf16[576,3072]{1,0:T(8,128)(2,1)} %get-tuple-element.277.refs_0_.refs_1_), channel_id=1, source_target_pairs={{0,16},{16,0},{1,17},{17,1},{2,18},{18,2},{3,19},{19,3},{4,20},{20... | collective-permute-start | bytes 10616840 | tf_op jit(solution)/shard_map/ppermute | solution.py:852
  130.5 18.7 %collective-permute-start.13 = (bf16[8,4,48,128]{3,2,1,0:T(8,128)(2,1)S(1)}, bf16[8,4,48,128]{3,2,1,0:T(8,128)(2,1)S(1)}, u32[]{:S(2)}, u32[]{:S(2)}) collective-permute-start(bf16[8,4,48,128]{3,2,1,0:T(8,128)(2,1)S(1)} %get-tuple-element.292), channel_id=1, source_target_pairs={{0,1},{1,0},{2,3},{3,2},{4,5},{5,4},{6,7},{7,6},{8,9},{9,8},{10,11... | collective-permute-start | bytes 1179656 | tf_op jit(solution)/shard_map/ppermute | solution.py:856
  147.0 32.4 %collective-permute-start.25 = (bf16[9,576,128]{2,1,0:T(8,128)(2,1)S(1)}, bf16[9,576,128]{2,1,0:T(8,128)(2,1)S(1)}, u32[]{:S(2)}, u32[]{:S(2)}) collective-permute-start(bf16[9,576,128]{2,1,0:T(8,128)(2,1)S(1)} %get-tuple-element.564), channel_id=1, source_target_pairs={{0,16},{16,0},{1,17},{17,1},{2,18},{18,2},{3,19},{19,3},{4,20},{20... | collective-permute-start | bytes 3981320 | tf_op jit(solution)/shard_map/ppermute | solution.py:852
  148.7 18.3 %collective-permute-start.10 = (bf16[8,1,192,128]{3,2,1,0:T(8,128)(2,1)S(1)}, bf16[8,1,192,128]{3,2,1,0:T(8,128)(2,1)S(1)}, u32[]{:S(2)}, u32[]{:S(2)}) collective-permute-start(bf16[8,1,192,128]{3,2,1,0:T(8,128)(2,1)S(1)} %get-tuple-element.288), channel_id=1, source_target_pairs={{0,4},{1,5},{2,6},{3,7},{4,0},{5,1},{6,2},{7,3},{8,12},{9,13},{10,... | collective-permute-start | bytes 1179656 | tf_op jit(solution)/shard_map/ppermute | solution.py:856
  176.3 56.5 %collective-permute-start.44 = (bf16[576,3072]{1,0:T(8,128)(2,1)S(1)}, bf16[576,3072]{1,0:T(8,128)(2,1)}, u32[]{:S(2)}, u32[]{:S(2)}) collective-permute-start(bf16[576,3072]{1,0:T(8,128)(2,1)S(1)} %copy-done.14), channel_id=1, source_target_pairs={{0,16},{16,0},{1,17},{17,1},{2,18},{18,2},{3,19},{19,3},{4,20},{20... | collective-permute-start | bytes 10616840 | tf_op jit(solution)/shard_map/ppermute | solution.py:852
  196.3 19.9 %collective-permute-start.26 = (bf16[2,1,192,128]{3,2,1,0:T(8,128)(2,1)S(1)}, bf16[2,1,192,128]{3,2,1,0:T(8,128)(2,1)S(1)}, u32[]{:S(2)}, u32[]{:S(2)}) collective-permute-start(bf16[2,1,192,128]{3,2,1,0:T(8,128)(2,1)S(1)} %get-tuple-element.319), channel_id=1, source_target_pairs={{0,4},{1,5},{2,6},{3,7},{4,0},{5,1},{6,2},{7,3},{8,12},{9,13},{10,... | collective-permute-start | bytes 294920 | tf_op jit(solution)/shard_map/ppermute | solution.py:856
  197.9 18.8 %collective-permute-start.27 = (bf16[2,1,192,128]{3,2,1,0:T(8,128)(2,1)S(1)}, bf16[2,1,192,128]{3,2,1,0:T(8,128)(2,1)S(1)}, u32[]{:S(2)}, u32[]{:S(2)}) collective-permute-start(bf16[2,1,192,128]{3,2,1,0:T(8,128)(2,1)S(1)} %get-tuple-element.321), channel_id=1, source_target_pairs={{0,4},{1,5},{2,6},{3,7},{4,0},{5,1},{6,2},{7,3},{8,12},{9,13},{10,... | collective-permute-start | bytes 294920 | tf_op jit(solution)/shard_map/ppermute | solution.py:856
  198.3 19.4 %collective-permute-start.28 = (bf16[2,1,192,128]{3,2,1,0:T(8,128)(2,1)S(1)}, bf16[2,1,192,128]{3,2,1,0:T(8,128)(2,1)S(1)}, u32[]{:S(2)}, u32[]{:S(2)}) collective-permute-start(bf16[2,1,192,128]{3,2,1,0:T(8,128)(2,1)S(1)} %get-tuple-element.323), channel_id=1, source_target_pairs={{0,2},{1,3},{2,0},{3,1},{4,6},{5,7},{6,4},{7,5},{8,10},{9,11},{10,... | collective-permute-start | bytes 294920 | tf_op jit(solution)/shard_map/ppermute | solution.py:856
  199.3 19.7 %collective-permute-start.29 = (bf16[2,4,48,128]{3,2,1,0:T(8,128)(2,1)S(1)}, bf16[2,4,48,128]{3,2,1,0:T(8,128)(2,1)S(1)}, u32[]{:S(2)}, u32[]{:S(2)}) collective-permute-start(bf16[2,4,48,128]{3,2,1,0:T(8,128)(2,1)S(1)} %get-tuple-element.325), channel_id=1, source_target_pairs={{0,4},{1,5},{2,6},{3,7},{4,0},{5,1},{6,2},{7,3},{8,12},{9,13},{10,... | collective-permute-start | bytes 294920 | tf_op jit(solution)/shard_map/ppermute | solution.py:856
  222.3 36.5 %collective-permute-start.50 = (bf16[576,1536]{1,0:T(8,128)(2,1)S(1)}, bf16[576,1536]{1,0:T(8,128)(2,1)S(1)}, u32[]{:S(2)}, u32[]{:S(2)}) collective-permute-start(bf16[576,1536]{1,0:T(8,128)(2,1)S(1)} %get-tuple-element.558), channel_id=1, source_target_pairs={{0,16},{16,0},{1,17},{17,1},{2,18},{18,2},{3,19},{19,3},{4,20},{20... | collective-permute-start | bytes 5308424 | tf_op jit(solution)/shard_map/ppermute | solution.py:852
  254.6 28.1 %collective-permute-start.54 = (bf16[8,1,192,128]{3,2,1,0:T(8,128)(2,1)S(1)}, bf16[8,1,192,128]{3,2,1,0:T(8,128)(2,1)S(1)}, u32[]{:S(2)}, u32[]{:S(2)}) collective-permute-start(bf16[8,1,192,128]{3,2,1,0:T(8,128)(2,1)S(1)} %get-tuple-element.378), channel_id=1, source_target_pairs={{0,1},{1,0},{2,3},{3,2},{4,5},{5,4},{6,7},{7,6},{8,9},{9,8},{10,11... | collective-permute-start | bytes 1179656 | tf_op jit(solution)/shard_map/ppermute | solution.py:856
  255.1 28.8 %collective-permute-start.55 = (bf16[8,1,192,128]{3,2,1,0:T(8,128)(2,1)S(1)}, bf16[8,1,192,128]{3,2,1,0:T(8,128)(2,1)S(1)}, u32[]{:S(2)}, u32[]{:S(2)}) collective-permute-start(bf16[8,1,192,128]{3,2,1,0:T(8,128)(2,1)S(1)} %get-tuple-element.380), channel_id=1, source_target_pairs={{0,2},{1,3},{2,0},{3,1},{4,6},{5,7},{6,4},{7,5},{8,10},{9,11},{10,... | collective-permute-start | bytes 1179656 | tf_op jit(solution)/shard_map/ppermute | solution.py:856
  265.3 20.3 %collective-permute-start.56 = (bf16[8,1,192,128]{3,2,1,0:T(8,128)(2,1)S(1)}, bf16[8,1,192,128]{3,2,1,0:T(8,128)(2,1)S(1)}, u32[]{:S(2)}, u32[]{:S(2)}) collective-permute-start(bf16[8,1,192,128]{3,2,1,0:T(8,128)(2,1)S(1)} %get-tuple-element.382), channel_id=1, source_target_pairs={{0,4},{1,5},{2,6},{3,7},{4,0},{5,1},{6,2},{7,3},{8,12},{9,13},{10,... | collective-permute-start | bytes 1179656 | tf_op jit(solution)/shard_map/ppermute | solution.py:856
  281.6 32.9 %collective-permute-start.71 = (bf16[9,576,128]{2,1,0:T(8,128)(2,1)S(1)}, bf16[9,576,128]{2,1,0:T(8,128)(2,1)S(1)}, u32[]{:S(2)}, u32[]{:S(2)}) collective-permute-start(bf16[9,576,128]{2,1,0:T(8,128)(2,1)S(1)} %get-tuple-element.562), channel_id=1, source_target_pairs={{0,16},{16,0},{1,17},{17,1},{2,18},{18,2},{3,19},{19,3},{4,20},{20... | collective-permute-start | bytes 3981320 | tf_op jit(solution)/shard_map/ppermute | solution.py:852
  322.1 18.3 %collective-permute-start.60 = (bf16[576,768]{1,0:T(8,128)(2,1)S(1)}, bf16[576,768]{1,0:T(8,128)(2,1)S(1)}, u32[]{:S(2)}, u32[]{:S(2)}) collective-permute-start(bf16[576,768]{1,0:T(8,128)(2,1)S(1)} %copy-done.18), channel_id=1, source_target_pairs={{16,0},{17,1},{18,2},{19,3},{20,4},{21,5},{22,6},{23,7},{24,8},{25... | collective-permute-start | bytes 2654216 | tf_op jit(solution)/shard_map/ppermute | solution.py:860
  345.7 48.3 %collective-permute-start.73 = (bf16[576,768]{1,0:T(8,128)(2,1)S(1)}, bf16[576,768]{1,0:T(8,128)(2,1)S(1)}, u32[]{:S(2)}, u32[]{:S(2)}) collective-permute-start(bf16[576,768]{1,0:T(8,128)(2,1)S(1)} %copy-done.20), channel_id=1, source_target_pairs={{0,16},{1,17},{2,18},{3,19},{4,20},{5,21},{6,22},{7,23},{8,24},{9,... | collective-permute-start | bytes 2654216 | tf_op jit(solution)/shard_map/ppermute | solution.py:860
  351.5 44.5 %collective-permute-start.72 = (bf16[576,768]{1,0:T(8,128)(2,1)S(1)}, bf16[576,768]{1,0:T(8,128)(2,1)S(1)}, u32[]{:S(2)}, u32[]{:S(2)}) collective-permute-start(bf16[576,768]{1,0:T(8,128)(2,1)S(1)} %get-tuple-element.419.refs_1_), channel_id=1, source_target_pairs={{16,0},{17,1},{18,2},{19,3},{20,4},{21,5},{22,6},{23,7},{24,8},{25... | collective-permute-start | bytes 2654216 | tf_op jit(solution)/shard_map/ppermute | solution.py:860
  363.5 19.8 %collective-permute-start.94 = (f32[10,32,128]{2,1,0:T(8,128)S(1)}, f32[10,32,128]{2,1,0:T(8,128)S(1)}, u32[]{:S(2)}, u32[]{:S(2)}) collective-permute-start(f32[10,32,128]{2,1,0:T(8,128)S(1)} %get-tuple-element.457.refs_18_), channel_id=1, source_target_pairs={{0,1},{1,0},{2,3},{3,2},{4,5},{5,4},{6,7},{7,6},{8,9},{9,8},{10,11... | collective-permute-start | bytes 491528 | tf_op jit(solution)/shard_map/ppermute | solution.py:856
  417.8 19.4 %collective-permute-start.111 = (f32[3,1,192,128]{3,2,1,0:T(8,128)}, f32[3,1,192,128]{3,2,1,0:T(8,128)}, u32[]{:S(2)}, u32[]{:S(2)}) collective-permute-start(f32[3,1,192,128]{3,2,1,0:T(8,128)} %copy-done.35), channel_id=1, source_target_pairs={{0,16},{1,17},{2,18},{3,19},{4,20},{5,21},{6,22},{7,23},{8,24},{9,... | collective-permute-start | bytes 884744 | tf_op jit(solution)/shard_map/ppermute | solution.py:860
  419.9 20.0 %collective-permute-start.112 = (f32[3,4,48,128]{3,2,1,0:T(8,128)}, f32[3,4,48,128]{3,2,1,0:T(8,128)}, u32[]{:S(2)}, u32[]{:S(2)}) collective-permute-start(f32[3,4,48,128]{3,2,1,0:T(8,128)} %copy-done.37), channel_id=1, source_target_pairs={{0,16},{1,17},{2,18},{3,19},{4,20},{5,21},{6,22},{7,23},{8,24},{9,... | collective-permute-start | bytes 884744 | tf_op jit(solution)/shard_map/ppermute | solution.py:860
  421.8 18.0 %collective-permute-start.113 = (f32[3,4,48,128]{3,2,1,0:T(8,128)}, f32[3,4,48,128]{3,2,1,0:T(8,128)}, u32[]{:S(2)}, u32[]{:S(2)}) collective-permute-start(f32[3,4,48,128]{3,2,1,0:T(8,128)} %copy-done.39), channel_id=1, source_target_pairs={{0,16},{1,17},{2,18},{3,19},{4,20},{5,21},{6,22},{7,23},{8,24},{9,... | collective-permute-start | bytes 884744 | tf_op jit(solution)/shard_map/ppermute | solution.py:860
  (195 other events, 1640.7 us)
